TPU v7x, 512 devices: a whole 4x8x8 slice. The times are simulated.
512 devices in a mesh: grp: 16 (over y, z_hi), dev: 32 (over x, z_lo, core).
Axes of the slice: x: 4, y: 8, z: 8 (z_hi: 2, z_lo: 4; z = z_hi * 4 + z_lo), core: 2. Of those that a mesh axis runs over, the one named last changes fastest.
Arguments:
- acts: bfloat16 [262144, 1024], P(('grp', 'dev')), may hold values from -48 to 48
- out_grads: bfloat16 [262144, 1024], P(('grp', 'dev')), may hold values from -0.01171875 to 0.01171875
- old_act_factor: float32 [1024, 1024], P('dev'), may hold values from -3 to 3
- old_grad_factor: float32 [1024, 1024], P('dev'), may hold values from -3 to 3
- act_basis: bfloat16 [1024, 1024], P('dev'), may hold values from -0.1875 to 0.1875
- grad_basis: bfloat16 [1024, 1024], P('dev'), may hold values from -0.1875 to 0.1875
- act_eigs: float32 [1024], P('dev'), may hold values from 0.3 to 3
- grad_eigs: float32 [1024], replicated, may hold values from 0.3 to 3
- sample_index: int32 [1024], P(('grp', 'dev')), may hold values from 0 to 511
Outputs:
- precond: float32 [1024, 1024], P('dev')
- act_factor: float32 [1024, 1024], P('dev')
- grad_factor: float32 [1024, 1024], P('dev')
Inputs may be any that keep to these rules, and one draw needn't show every extreme that they name: `sample_index`: every entry indexes a token of the device that holds the entry.
All inputs are finite; a program needn't handle non-finite values.
Results may differ from a plain program's by a relative error of at most 0.0059.
Values may be sent and summed in bfloat16 or wider, within the bound.
A program may use at most 64 MiB of HBM per device.

v0:
```python
import jax
import jax.numpy as jnp
from jax import lax
from jax.sharding import PartitionSpec as P


def contract_first(left_side, right_side):
    return lax.dot_general(
        left_side, right_side, (((0,), (0,)), ((), ())), preferred_element_type=jnp.float32
    )


def contract_last(left_side, right_side):
    return lax.dot_general(
        left_side, right_side, (((1,), (1,)), ((), ())), preferred_element_type=jnp.float32
    )


def factor_rows(all_acts, all_grads, row_start, shard_rows):
    act_part = contract_first(
        lax.dynamic_slice_in_dim(all_acts, row_start, shard_rows, 1), all_acts
    )
    grad_part = contract_first(
        lax.dynamic_slice_in_dim(all_grads, row_start, shard_rows, 1), all_grads
    )
    return (act_part, grad_part)


def local(
    acts,
    out_grads,
    old_act_factor,
    old_grad_factor,
    act_basis,
    grad_basis,
    act_eigs,
    grad_eigs,
    sample_index,
):
    shard_rows = old_act_factor.shape[0]
    row_start = lax.axis_index("dev") * shard_rows
    projected = jnp.dot(
        acts,
        lax.all_gather(act_basis, "dev", axis=0, tiled=True),
        preferred_element_type=jnp.float32,
    ).astype(jnp.bfloat16)
    group_sum = lax.psum_scatter(
        contract_first(projected, out_grads), "dev", scatter_dimension=0, tiled=True
    )
    rotated = lax.psum(group_sum, "grp").astype(jnp.bfloat16)
    picked_acts = jnp.take(acts, sample_index, axis=0)
    picked_grads = jnp.take(out_grads, sample_index, axis=0)
    all_acts, all_grads = (
        lax.all_gather(picked_acts, "dev", axis=0, tiled=True),
        lax.all_gather(picked_grads, "dev", axis=0, tiled=True),
    )
    act_part, grad_part = factor_rows(all_acts, all_grads, row_start, shard_rows)
    act_stat, grad_stat = lax.psum((act_part, grad_part), "grp")
    device_count = lax.axis_size("grp") * lax.axis_size("dev")
    total_samples = device_count * sample_index.shape[0]
    total_tokens = device_count * acts.shape[0]
    act_factor = 0.75 * old_act_factor + 0.25 / total_samples * act_stat
    grad_factor = 0.75 * old_grad_factor + 0.25 * total_tokens / total_samples * grad_stat
    divisor = act_eigs[:, None] * grad_eigs[None, :] + 0.1
    whole_basis = lax.all_gather(grad_basis, "dev", axis=0, tiled=True)
    turned = jnp.dot(rotated, whole_basis, preferred_element_type=jnp.float32)
    scaled = (turned / divisor).astype(jnp.bfloat16)
    restored = contract_last(scaled, whole_basis).astype(jnp.bfloat16)
    precond = jnp.dot(
        act_basis,
        lax.all_gather(restored, "dev", axis=0, tiled=True),
        preferred_element_type=jnp.float32,
    )
    return (precond, act_factor, grad_factor)


def solution(mesh):
    return jax.shard_map(
        local,
        mesh=mesh,
        in_specs=(
            P(("grp", "dev"), None),
            P(("grp", "dev"), None),
            P("dev", None),
            P("dev", None),
            P("dev", None),
            P("dev", None),
            P("dev"),
            P(),
            P(("grp", "dev")),
        ),
        out_specs=(P("dev", None), P("dev", None), P("dev", None)),
        check_vma=False,
    )
```

profile of v0, /device:TPU:1, one launch (start us, length us, event | category | flops | bytes accessed | tf_op | source)
XLA Modules:
  0.0 409.8 jit_solution(16849122765873956781)
XLA Ops:
  8.1 0.7 all-gather.6.cloned.1.call-update
  8.7 0.0 reduce-scatter.2.cloned.1.call-start
  8.8 71.4 %all-gather.6.cloned.1.call-done = bf16[1024,1024]{1,0:T(8,128)(2,1)} async-done(((bf16[32,1024]{1,0:T(8,128)(2,1)}), bf16[1024,1024]{1,0:T(8,128)(2,1)}) %all-gather.6.cloned.1.call-update) | async-done | bytes 2097168 | tf_op jit(solution)/shard_map/all_gather | solution.py:44
  80.2 6.2 %fusion.1 = f32[1024,1024]{1,0:T(8,128)} fusion(bf16[512,1024]{1,0:T(8,128)(2,1)} %param.12, bf16[512,1024]{1,0:T(8,128)(2,1)S(1)} %copy-done, bf16[1024,1024]{1,0:T(8,128)(2,1)} %all-gather.6.cloned.1.call-done), kind=kOutput, calls=%fused_computation.7 | convolution fusion | flops 2148007936 | bytes 8388608 | tf_op jit(solution)/shard_map/dot_general | solution.py:8
  86.3 0.0 all-gather.8.cloned.1.call-start
  86.4 0.7 all-gather.8.cloned.1.call-update
  87.1 0.0 all-reduce.4.cloned.1.call-start
  87.2 0.6 gather_fusion
  87.7 1.9 gather_fusion.1
  89.7 0.1 fusion.14
  89.8 41.6 %all-gather = bf16[32,2,1024]{2,1,0:T(2,128)(2,1)S(1)} all-gather(bf16[1,2,1024]{2,1,0:T(2,128)(2,1)S(1)} %get-tuple-element.7), channel_id=1, replica_groups=mesh['grp'=16,'dev'=32] {'dev'}, dimensions={0}, use_global_device_ids=true | all-gather | bytes 135168 | tf_op jit(solution)/shard_map/all_gather | solution.py:54
  131.4 0.1 reshape.32
  131.4 38.6 %all-gather.1 = bf16[32,2,1024]{2,1,0:T(2,128)(2,1)S(1)} all-gather(bf16[1,2,1024]{2,1,0:T(2,128)(2,1)S(1)} %get-tuple-element.6), channel_id=1, replica_groups=mesh['grp'=16,'dev'=32] {'dev'}, dimensions={0}, use_global_device_ids=true | all-gather | bytes 135168 | tf_op jit(solution)/shard_map/all_gather | solution.py:55
  170.1 0.1 reshape.34
  170.1 0.9 fusion.11
  171.0 0.9 fusion.9
  172.0 0.0 all-gather.10.cloned.1.call-start
  172.0 65.0 %reduce-scatter.2.cloned.1.call-done = f32[32,1024]{1,0:T(8,128)} async-done(((f32[1024,1024]{1,0:T(8,128)}), f32[32,1024]{1,0:T(8,128)}) %reduce-scatter.2.cloned.1.call-update) | async-done | bytes 131088 | tf_op jit(solution)/shard_map/reduce_scatter | solution.py:47
  237.1 87.5 %all-reduce.5 = bf16[32,1024]{1,0:T(8,128)(2,1)S(1)} all-reduce(f32[32,1024]{1,0:T(8,128)} %reduce-scatter.2.cloned.1.call-done), channel_id=1, replica_groups=mesh['grp'=16,'dev'=32] {'grp'}, use_global_device_ids=true, to_apply=%region_1.0 | all-reduce | flops 32768 | bytes 196608 | tf_op jit(solution)/shard_map/psum | solution.py:50
  324.7 4.0 convolution_convert_fusion.1
  328.7 28.5 %all-reduce.4.cloned.1.call-done = (f32[32,1024]{1,0:T(8,128)}, f32[32,1024]{1,0:T(8,128)}) async-done(((f32[32,1024]{1,0:T(8,128)}, f32[32,1024]{1,0:T(8,128)}), (f32[32,1024]{1,0:T(8,128)}, f32[32,1024]{1,0:T(8,128)})) %all-reduce.4.cloned.1.call-update) | async-done | bytes 262160 | tf_op jit(solution)/shard_map/psum | solution.py:58
  357.2 1.7 multiply_add_fusion
  358.9 41.0 %all-gather.10.cloned.1.call-done = bf16[1024,1024]{1,0:T(8,128)(2,1)} async-done(((bf16[32,1024]{1,0:T(8,128)(2,1)}), bf16[1024,1024]{1,0:T(8,128)(2,1)}) %all-gather.10.cloned.1.call-update) | async-done | bytes 2097168 | tf_op jit(solution)/shard_map/all_gather | solution.py:71
  399.9 2.7 convolution_bitcast_fusion
  (22 shorter events, 0.2 us)
Async XLA Ops:
  8.0 72.2 %copy-start = (bf16[512,1024]{1,0:T(8,128)(2,1)S(1)}, bf16[512,1024]{1,0:T(8,128)(2,1)}, u32[]{:S(2)}) copy-start(bf16[512,1024]{1,0:T(8,128)(2,1)} %param.11) | copy-start | bytes 3145732
  8.0 72.1 %all-gather.6.cloned.1.call-start = ((), (), s32[]{:S(2)}) async-start(), calls=%async_computation.1 | async-start | bytes 2162688 | tf_op jit(solution)/shard_map/all_gather | solution.py:44
  8.7 228.3 %reduce-scatter.2.cloned.1.call-start = ((), (), s32[]{:S(2)}) async-start(), calls=%async_computation.2 | async-start | bytes 4325376 | tf_op jit(solution)/shard_map/reduce_scatter | solution.py:47
  86.3 0.8 copy-start.6
  86.3 238.4 %copy-start.4 = (f32[1024]{0:T(1024)S(1)}, f32[1024]{0:T(1024)}, u32[]{:S(2)}) copy-start(f32[1024]{0:T(1024)} %param.18) | copy-start | bytes 12292
  86.3 238.4 %copy-start.5 = (f32[32]{0:T(128)S(1)}, f32[32]{0:T(128)}, u32[]{:S(2)}) copy-start(f32[32]{0:T(128)} %param.17) | copy-start | bytes 388
  86.3 238.3 %all-gather.8.cloned.1.call-start = ((), (), s32[]{:S(2)}) async-start(), calls=%async_computation.3 | async-start | bytes 2162688 | tf_op jit(solution)/shard_map/all_gather | solution.py:65
  87.1 270.1 %all-reduce.4.cloned.1.call-start = ((), (), s32[]{:S(2)}) async-start(), calls=%async_computation.5 | async-start | bytes 524288 | tf_op jit(solution)/shard_map/psum | solution.py:58
  172.0 228.0 %all-gather.10.cloned.1.call-start = ((), (), s32[]{:S(2)}) async-start(), calls=%async_computation.4 | async-start | bytes 2162688 | tf_op jit(solution)/shard_map/all_gather | solution.py:71
  324.6 32.6 %copy-start.2 = (f32[32,1024]{1,0:T(8,128)S(1)}, f32[32,1024]{1,0:T(8,128)}, u32[]{:S(2)}) copy-start(f32[32,1024]{1,0:T(8,128)} %param.14) | copy-start | bytes 393220
  324.6 32.6 %copy-start.3 = (f32[32,1024]{1,0:T(8,128)S(1)}, f32[32,1024]{1,0:T(8,128)}, u32[]{:S(2)}) copy-start(f32[32,1024]{1,0:T(8,128)} %param.13) | copy-start | bytes 393220
  324.6 75.3 %copy-start.1 = (bf16[32,1024]{1,0:T(8,128)(2,1)S(1)}, bf16[32,1024]{1,0:T(8,128)(2,1)}, u32[]{:S(2)}) copy-start(bf16[32,1024]{1,0:T(8,128)(2,1)} %param.15) | copy-start | bytes 196612
Sparse Core Ops, SparseCore 0:
  11.0 69.1 all-gather.5
  86.5 150.5 reduce-scatter.1
  239.2 65.0 all-gather.7
  328.9 71.0 all-gather.9
Sparse Core Ops, SparseCore 1:
  172.1 185.1 all-reduce.3
where the time goes:
time: 410 us
  waiting for transfers between devices  207 us (50%)
  blocking collectives  168 us (41%)
  between operations  15.3 us (4%)
  matrix products  14.7 us (4%)
    psum x1, blocking collectives, local(): rotated = lax.psum(group_sum, 'grp').astype(jnp.bfloat16)  87.5 us
    all_gather x1, waiting for transfers between devices, local(): lax.all_gather(act_basis, 'dev', axis=0, tiled=True)  71.4 us
    reduce_scatter x1, waiting for transfers between devices, local(): lax.psum_scatter(contract_first(projected, out_grads), 'dev', scatter_dim...  65 us
    all_gather x1, blocking collectives, local(): lax.all_gather(picked_acts, 'dev', axis=0, tiled=True)  41.6 us
    all_gather x1, waiting for transfers between devices, local(): lax.all_gather(restored, 'dev', axis=0, tiled=True)  41 us
    all_gather x1, blocking collectives, local(): lax.all_gather(picked_grads, 'dev', axis=0, tiled=True)  38.6 us
    psum x1, waiting for transfers between devices, local(): act_stat, grad_stat = lax.psum((act_part, grad_part), 'grp')  28.5 us
  transfers between devices with their start and end apart: 5, of which 4 were waited for; matrix products, arithmetic and copies ran while one was open for 3% of the time, Pallas kernels for 0%

commit v1 on v0

v1 whole, which is shorter than its diff:
```python
import functools

import jax
import jax.numpy as jnp
from jax import lax
from jax.experimental import pallas as pl
from jax.experimental.pallas import tpu as pltpu
from jax.sharding import PartitionSpec as P

NX, NY, NZ, ZL = 4, 8, 8, 4
D, TOK = 1024, 512
HALF = D // 2
CHUNKS, CW = 4, 256
BF, F32 = jnp.bfloat16, jnp.float32
DX = (1, 3, 2)
DY = (1, 7, 2, 6, 3, 5, 4)
DZ = (1, 7, 2, 6, 3, 5, 4)
DZL = (1, 7, 2)
DXC = tuple((dx, dc) for dx in (0, 1, 3, 2) for dc in (0, 1) if (dx, dc) != (0, 0))


def dot(left, right, dims=(((1,), (0,)), ((), ()))):
    return lax.dot_general(left, right, dims, preferred_element_type=F32)


def kernel(
    idx_hbm, acts_ref, grads_ref, a_hbm, b_ref, aeig_hbm, geig_hbm,
    out_ref,
    idx_ref, a_ref, aeig_ref, geig_ref,
    acts_v, grads_v, aperm, abuf, projt,
    tbuf, sendx1, recvx1, sendx2, recvx2, sendz, recvz, sendy, recvy,
    bcol, tsend, trecv, rbuf, obuf,
    picks, pbuf, pwide, xbuf, sfull, ssend, srecv, szsend, szrecv, sout,
    lsem, ssem, rsem,
):
    grp, dev = lax.axis_index("grp"), lax.axis_index("dev")
    y, zh = grp // 2, grp % 2
    x, zl, c = dev // 8, (dev // 2) % 4, dev % 2
    z = zh * ZL + zl

    def at(px, py, pz, pc):
        return {"grp": py * 2 + pz // ZL, "dev": px * 8 + (pz % ZL) * 2 + pc}

    def to_x(step):
        return at((x + step) % NX, y, z, c)

    def to_y(step):
        return at(x, (y + step) % NY, z, c)

    def to_z(step):
        return at(x, y, (z + step) % NZ, c)

    def to_xc(step):
        return at((x + step[0]) % NX, y, z, (c + step[1]) % 2)

    sibling = at(x, y, z, 1 - c)
    slot_z = (z % ZL) * 2 + z // ZL

    counter = [0]
    pending = []

    def send(moves, like):
        n = counter[0]
        counter[0] += 1

        def copy(src, dst, target):
            return pltpu.make_async_remote_copy(
                src_ref=src, dst_ref=dst, send_sem=ssem.at[n], recv_sem=rsem.at[n],
                device_id=target, device_id_type=pl.DeviceIdType.MESH,
            )

        for move in moves:
            copy(*move).start()
        whole = copy(like, like, sibling)
        pending.append(whole)
        return whole

    def gather(ref, targets, like):
        return send([(ref, ref, target) for target in targets], like)

    def drain():
        for copy in pending:
            copy.wait_send()
        pending.clear()

    all_x = [to_x(s) for s in DX]
    all_y = [to_y(s) for s in DY]
    all_z = [to_z(s) for s in DZ]
    all_zl = [to_z(s) for s in DZL]
    all_xc = [to_xc(s) for s in DXC]
    x_up, x_down, x_far = (x + 1) % NX, (x + 3) % NX, (x + 2) % NX
    zl_up, zl_down = (zl + 1) % ZL, (zl + 3) % ZL

    barrier = pltpu.get_barrier_semaphore()
    partners = all_xc + all_y + all_z
    for partner in partners:
        pl.semaphore_signal(
            barrier, inc=1, device_id=partner, device_id_type=pl.DeviceIdType.MESH
        )

    own = [
        pltpu.make_async_copy(src, dst, lsem.at[i])
        for i, (src, dst) in enumerate((
            (a_hbm, a_ref), (idx_hbm, idx_ref), (acts_ref, acts_v.at[0]), (grads_ref, grads_v.at[0]),
            (aeig_hbm, aeig_ref),
            (geig_hbm.at[:, pl.ds(pl.multiple_of(y * 128, 128), 128)], geig_ref),
        ))
    ]
    own_basis = [
        pltpu.make_async_copy(
            b_ref.at[:, pl.ds(pl.multiple_of(y * 128, 128), 128)], bcol.at[x, zl, c], lsem.at[6]
        )
    ]
    for copy in own + own_basis:
        copy.start()

    own[0].wait()
    lane_block = lax.broadcasted_iota(jnp.int32, (32, 128), 1) // 32
    for m in range(4):
        u = a_ref[:, 256 * m:256 * m + 128].astype(F32)
        v = a_ref[:, 256 * m + 128:256 * m + 256].astype(F32)
        even = jnp.where(
            lane_block == 0, u,
            jnp.where(lane_block == 1, pltpu.roll(u, 96, 1),
                      jnp.where(lane_block == 2, pltpu.roll(v, 64, 1), pltpu.roll(v, 32, 1))),
        )
        odd = jnp.where(
            lane_block == 0, pltpu.roll(u, 96, 1),
            jnp.where(lane_block == 1, pltpu.roll(u, 64, 1),
                      jnp.where(lane_block == 2, pltpu.roll(v, 32, 1), v)),
        )
        cols = slice(128 * (m % 2), 128 * (m % 2) + 128)
        aperm[0, m // 2, :, cols] = even.astype(BF)
        aperm[1, m // 2, :, cols] = odd.astype(BF)
    my_rows = pl.ds(pl.multiple_of(c * 32, 32), 32)
    abuf[:, x, zl, my_rows, :] = aperm[c]
    pl.semaphore_wait(barrier, len(partners))

    mine = abuf.at[:, x, zl, my_rows, :]
    a_sib = send([(aperm.at[1 - c], mine, sibling)], mine)
    acts_sib = send([(acts_ref, acts_v.at[1], sibling)], acts_v.at[1])
    grads_sib = send([(grads_ref, grads_v.at[1], sibling)], grads_v.at[1])

    a_sib.wait_recv()
    az1 = gather(abuf.at[0, x, zl], all_zl, abuf.at[0, 0, pl.ds(0, 3)])
    ax1 = gather(abuf.at[1, x, zl], all_x, abuf.at[0, 0, pl.ds(0, 3)])

    for copy in own[1:]:
        copy.wait()
    row = lax.broadcasted_iota(jnp.int32, (16, TOK), 0)
    col = lax.broadcasted_iota(jnp.int32, (16, TOK), 1)
    wanted = jnp.where(row == 0, idx_ref[0, 0], jnp.where(row == 1, idx_ref[0, 1], -1))
    hot = jnp.where(col == wanted, 1.0, 0.0).astype(BF)
    for i, source in enumerate((acts_v, grads_v)):
        rows = dot(hot, source[0])
        for s in range(2):
            for k in range(8):
                picks[i, s * 8 + k:s * 8 + k + 1, :] = rows[s:s + 1, 128 * k:128 * k + 128]
    pbuf[c, x, zl] = picks[...].astype(BF)
    pz = gather(pbuf.at[c, x, zl], all_zl, pbuf.at[0, 0, pl.ds(0, 3)])
    for copy in own_basis:
        copy.wait()
    bz = gather(bcol.at[x, zl, c], all_zl, bcol.at[0, pl.ds(0, 3), 0])

    az1.wait_recv()
    mine = abuf.at[0, x]
    ax2 = [send([(mine, mine, to_x(s))], mine) for s in (1, 3)]
    ax1.wait_recv()
    mine = abuf.at[1, :, zl]
    az2 = [send([(mine, mine, to_z(s))], mine) for s in (1, 7)]
    pz.wait_recv()
    px = gather(pbuf.at[c, x], all_x, pbuf.at[0, pl.ds(0, 3)])
    bz.wait_recv()
    bx = gather(bcol.at[x, :, c], all_x, bcol.at[pl.ds(0, 3), :, 0])

    a3 = []
    for block, target, copy in (
        (abuf.at[0, x_down, pl.ds(0, 2)], to_x(1), ax2[0]),
        (abuf.at[0, x_up, pl.ds(2, 2)], to_x(3), ax2[1]),
        (abuf.at[1, pl.ds(0, 2), zl_down], to_z(1), az2[0]),
        (abuf.at[1, pl.ds(2, 2), zl_up], to_z(7), az2[1]),
    ):
        copy.wait_recv()
        a3.append(send([(block, block, target)], block))

    acts_sib.wait_recv()
    for copy in a3:
        copy.wait_recv()

    for slot in range(2):
        for t in range(2):
            tokens = acts_v[slot, 256 * t:256 * t + 256, :]
            for h in range(2):
                proj = dot(tokens, abuf[h].reshape(D, 256)).astype(BF)
                projt[256 * h:256 * h + 256, slot * TOK + 256 * t:slot * TOK + 256 * t + 256] = proj.T

    grads_sib.wait_recv()
    r1, r2 = {}, {}

    def forward(j):
        r1[j][0].wait_recv()
        sendx2[j, 0] = (tbuf[j, x_up, 0:64, :] + recvx1[j, 0, 0].astype(F32)).astype(BF)
        up = send([(sendx2.at[j, 0], recvx2.at[j, 0], to_x(1))], recvx2.at[j, 0])
        r1[j][1].wait_recv()
        sendx2[j, 1] = (tbuf[j, x_down, 64:128, :] + recvx1[j, 1, 0].astype(F32)).astype(BF)
        down = send([(sendx2.at[j, 1], recvx2.at[j, 1], to_x(3))], recvx2.at[j, 1])
        r2[j] = (up, down)

    for j in range(CHUNKS):
        cols = slice(CW * j, CW * j + CW)
        term = dot(projt[:, 0:TOK], grads_v[0, :, cols])
        term = term + dot(projt[:, TOK:], grads_v[1, :, cols])
        tbuf[j] = term.reshape(NX, 128, CW)
        sendx1[j, 0, 0] = tbuf[j, x_far, 0:64, :].astype(BF)
        sendx1[j, 0, 1] = tbuf[j, x_up, 64:128, :].astype(BF)
        sendx1[j, 1, 0] = tbuf[j, x_far, 64:128, :].astype(BF)
        sendx1[j, 1, 1] = tbuf[j, x_down, 0:64, :].astype(BF)
        r1[j] = [
            send([(sendx1.at[j, i], recvx1.at[j, i], to_x(s))], recvx1.at[j, i])
            for i, s in enumerate((1, 3))
        ]
        if j > 1:
            forward(j - 2)
    forward(CHUNKS - 2)
    forward(CHUNKS - 1)

    px.wait_recv()
    psib = gather(pbuf.at[c], [sibling], pbuf.at[c])
    bx.wait_recv()
    bsib = gather(bcol.at[:, :, c], [sibling], bcol.at[:, :, c])

    psib.wait_recv()
    for i in range(2):
        pwide[...] = pbuf[:, :, :, i].reshape(2 * NX * ZL * 16, 128).astype(F32)
        for k in range(8):
            part = jnp.concatenate(
                [pwide[pl.ds(s * 8 + k, 2 * NX * ZL, stride=16), :] for s in range(2)], axis=0
            )
            xbuf[k] = part.astype(BF)
        wide = jnp.concatenate([xbuf[k] for k in range(8)], axis=1)
        sfull[...] = dot(xbuf[dev // 4], wide, (((0,), (0,)), ((), ())))
        rows = sfull[pl.ds(pl.multiple_of((dev % 4) * 32, 32), 32), :]
        for k in range(8):
            ssend[k, i] = rows[:, 128 * k:128 * k + 128].astype(BF)
    sy = send([(ssend.at[(y + s) % NY], srecv.at[i], to_y(s)) for i, s in enumerate(DY)], srecv)

    rz, ry = {}, {}

    def sum_x(j):
        r2[j][0].wait_recv()
        r2[j][1].wait_recv()
        top = tbuf[j, x, 0:64, :] + recvx1[j, 1, 1].astype(F32) + recvx2[j, 0].astype(F32)
        low = tbuf[j, x, 64:128, :] + recvx1[j, 0, 1].astype(F32) + recvx2[j, 1].astype(F32)
        sendz[j, 0:4] = top.astype(BF).reshape(4, 16, CW)
        sendz[j, 4:8] = low.astype(BF).reshape(4, 16, CW)
        moves = []
        for i, s in enumerate(DZ):
            to = (z + s) % NZ
            moves.append((sendz.at[j, (to % ZL) * 2 + to // ZL], recvz.at[j, i], to_z(s)))
        rz[j] = send(moves, recvz.at[j])

    def sum_z(j):
        rz[j].wait_recv()
        total = sendz[j, slot_z].astype(F32)
        for i in range(len(DZ)):
            total = total + recvz[j, i].astype(F32)
        sendy[j] = total.astype(BF)
        ry[j] = send(
            [(sendy.at[j], recvy.at[j, i], to_y(s)) for i, s in enumerate(DY)], recvy.at[j]
        )

    sum_x(0)
    for j in range(1, CHUNKS):
        sum_x(j)
        sum_z(j - 1)
    sum_z(CHUNKS - 1)

    sy.wait_recv()
    stat = ssend[y].astype(F32)
    for i in range(len(DY)):
        stat = stat + srecv[i].astype(F32)
    szsend[...] = stat
    sz = send([(szsend, szrecv, to_z(4))], szrecv)
    sz.wait_recv()
    sout[y] = (szsend[...] + szrecv[...]).astype(BF)
    so = gather(sout.at[y], all_y, sout.at[pl.ds(0, 7)])

    lane = lax.broadcasted_iota(jnp.int32, (16, 32), 1)
    sub = lax.broadcasted_iota(jnp.int32, (16, 32), 0)
    eigs = jnp.sum(
        jnp.where(lane == sub + 16 * zh, aeig_ref[...], 0.0), axis=1, keepdims=True
    )
    divisor = eigs * geig_ref[...] + 0.1
    bsib.wait_recv()
    basis = bcol[...].reshape(D, 128)
    parts = []
    for j in range(CHUNKS):
        ry[j].wait_recv()
        total = sendy[j].astype(F32)
        for i in range(len(DY)):
            total = total + recvy[j, i].astype(F32)
        parts.append(total.astype(BF))
    turned = dot(jnp.concatenate(parts, axis=1), basis)
    scaled = (turned / divisor).astype(BF)
    partial = dot(scaled, basis, (((1,), (1,)), ((), ())))
    for k in range(8):
        tsend[k] = partial[:, 128 * k:128 * k + 128]
    ty = send([(tsend.at[(y + s) % NY], trecv.at[i], to_y(s)) for i, s in enumerate(DY)], trecv)
    ty.wait_recv()
    restored = tsend[y]
    for i in range(len(DY)):
        restored = restored + trecv[i]
    rbuf[c * NX + x, slot_z] = restored.astype(BF)
    mine = rbuf.at[c * NX + x]
    rzg = gather(mine.at[slot_z], all_z, rbuf.at[0, pl.ds(0, 7)])
    rzg.wait_recv()
    rxc = gather(mine, all_xc, rbuf.at[pl.ds(0, 7)])

    so.wait_recv()
    for i in range(2):
        for k in range(8):
            out_ref[1 + i, :, 128 * k:128 * k + 128] = sout[k, i]
    rxc.wait_recv()
    total = jnp.zeros((32, 128), F32)
    for half in range(2):
        for h in range(2):
            total = total + dot(aperm[half, h], rbuf[half * NX + 2 * h:half * NX + 2 * h + 2].reshape(256, 128))
    obuf[y] = total.astype(BF)
    po = gather(obuf.at[y], all_y, obuf.at[pl.ds(0, 7)])

    drain()

    po.wait_recv()
    for k in range(8):
        out_ref[0, :, 128 * k:128 * k + 128] = obuf[k]


def finish(result_ref, old_act_ref, old_grad_ref, pre_ref, act_ref, grad_ref, *, act_scale, grad_scale):
    pre_ref[...] = result_ref[0].astype(F32)
    act_ref[...] = 0.75 * old_act_ref[...] + act_scale * result_ref[1].astype(F32)
    grad_ref[...] = 0.75 * old_grad_ref[...] + grad_scale * result_ref[2].astype(F32)


def local(
    acts,
    out_grads,
    old_act_factor,
    old_grad_factor,
    act_basis,
    grad_basis,
    act_eigs,
    grad_eigs,
    sample_index,
):
    vmem = pl.BlockSpec(memory_space=pltpu.VMEM)
    hbm = pl.BlockSpec(memory_space=pl.ANY)
    copies = 64
    result = pl.pallas_call(
        kernel,
        out_shape=jax.ShapeDtypeStruct((3, 32, D), BF),
        in_specs=[hbm] * 7,
        out_specs=vmem,
        scratch_shapes=[
            pltpu.SMEM((1, 2), jnp.int32),
            pltpu.VMEM((32, D), BF),
            pltpu.VMEM((1, 32), F32),
            pltpu.VMEM((1, 128), F32),
            pltpu.VMEM((2, TOK, D), BF),
            pltpu.VMEM((2, TOK, D), BF),
            pltpu.VMEM((2, 2, 32, 256), BF),
            pltpu.VMEM((2, NX, ZL, 64, 256), BF),
            pltpu.VMEM((HALF, 2 * TOK), BF),
            pltpu.VMEM((CHUNKS, NX, 128, CW), F32),
            pltpu.VMEM((CHUNKS, 2, 2, 64, CW), BF),
            pltpu.VMEM((CHUNKS, 2, 2, 64, CW), BF),
            pltpu.VMEM((CHUNKS, 2, 64, CW), BF),
            pltpu.VMEM((CHUNKS, 2, 64, CW), BF),
            pltpu.VMEM((CHUNKS, NZ, 16, CW), BF),
            pltpu.VMEM((CHUNKS, 7, 16, CW), BF),
            pltpu.VMEM((CHUNKS, 16, CW), BF),
            pltpu.VMEM((CHUNKS, 7, 16, CW), BF),
            pltpu.VMEM((NX, ZL, 2, 32, 128), BF),
            pltpu.VMEM((NY, 16, 128), F32),
            pltpu.VMEM((7, 16, 128), F32),
            pltpu.VMEM((2 * NX, NZ, 16, 128), BF),
            pltpu.VMEM((NY, 32, 128), BF),
            pltpu.VMEM((2, 16, 128), F32),
            pltpu.VMEM((2, NX, ZL, 2, 16, 128), BF),
            pltpu.VMEM((2 * NX * ZL * 16, 128), F32),
            pltpu.VMEM((8, 64, 128), BF),
            pltpu.VMEM((128, D), F32),
            pltpu.VMEM((NY, 2, 32, 128), BF),
            pltpu.VMEM((7, 2, 32, 128), BF),
            pltpu.VMEM((2, 32, 128), F32),
            pltpu.VMEM((2, 32, 128), F32),
            pltpu.VMEM((NY, 2, 32, 128), BF),
            pltpu.SemaphoreType.DMA((7,)),
            pltpu.SemaphoreType.DMA((copies,)),
            pltpu.SemaphoreType.DMA((copies,)),
        ],
        compiler_params=pltpu.CompilerParams(
            collective_id=0, has_side_effects=True, vmem_limit_bytes=63 * 1024 * 1024
        ),
        cost_estimate=pl.CostEstimate(
            flops=4 * TOK * D * D, bytes_accessed=4 * TOK * D, transcendentals=0
        ),
    )(
        sample_index.reshape(1, 2), acts, out_grads, act_basis, grad_basis,
        act_eigs.reshape(1, 32), grad_eigs.reshape(1, D),
    )
    device_count = lax.axis_size("grp") * lax.axis_size("dev")
    total_samples = device_count * sample_index.shape[0]
    total_tokens = device_count * acts.shape[0]
    return pl.pallas_call(
        functools.partial(
            finish,
            act_scale=0.25 / total_samples,
            grad_scale=0.25 * total_tokens / total_samples,
        ),
        out_shape=(jax.ShapeDtypeStruct((32, D), F32),) * 3,
        in_specs=[vmem] * 3,
        out_specs=(vmem,) * 3,
    )(result, old_act_factor, old_grad_factor)


def solution(mesh):
    return jax.shard_map(
        local,
        mesh=mesh,
        in_specs=(
            P(("grp", "dev"), None),
            P(("grp", "dev"), None),
            P("dev", None),
            P("dev", None),
            P("dev", None),
            P("dev", None),
            P("dev"),
            P(),
            P(("grp", "dev")),
        ),
        out_specs=(P("dev", None), P("dev", None), P("dev", None)),
        check_vma=False,
    )
```

time: 410 us -> 86.9 us (0.21)
  waiting for transfers between devices: 207 us -> 0 us
  blocking collectives: 168 us -> 0 us
  Pallas kernels: 0 us -> 86.1 us
  matrix products: 14.7 us -> 0 us
  between operations: 15.3 us -> 0.64 us
    all_gather x3 -> x0, waiting for transfers between devices: 112 us -> none  [the longest x1 71.4 us: local(): lax.all_gather(act_basis, 'dev', axis=0, tiled=True)]
    psum x1 -> x0, blocking collectives: 87.5 us -> none  [local(): rotated = lax.psum(group_sum, 'grp').astype(jnp.bfloat16)]
    pallas_call x0 -> x2, Pallas kernels: none -> 86.1 us  [the longest x1 84.3 us: local(): pl.pallas_call(kernel, out_shape=jax.ShapeDtypeStruct((3, 32, D), BF), in...]
    all_gather x2 -> x0, blocking collectives: 80.2 us -> none  [the longest x1 41.6 us: local(): lax.all_gather(picked_acts, 'dev', axis=0, tiled=True)]
    reduce_scatter x1 -> x0, waiting for transfers between devices: 65 us -> none  [local(): lax.psum_scatter(contract_first(projected, out_grads), 'dev', scatter_dim...]
    psum x1 -> x0, waiting for transfers between devices: 28.5 us -> none  [local(): act_stat, grad_stat = lax.psum((act_part, grad_part), 'grp')]
    dot_general x5 -> x0, matrix products: 14.7 us -> none  [the longest x3 8 us: contract_first(): lax.dot_general(left_side, right_side, (((0,), (0,)), ((), ())), preferre...]
  transfers between devices with their start and end apart: 5 -> 0, of which waited for: 4 -> 0; matrix products, arithmetic and copies ran while one was open for 3% -> 0% of each run, Pallas kernels for 0% -> 0%
where the time goes in v1:
time: 86.9 us; the launch traced here: 86.7 us
  Pallas kernels  86.1 us (99%)
    pallas_call x1, Pallas kernels, local(): pl.pallas_call(kernel, out_shape=jax.ShapeDtypeStruct((3, 32, D), BF), in...  84.3 us
    pallas_call x1, Pallas kernels, local(): pl.pallas_call(functools.partial(finish, act_scale=0.25 / total_samples,...  1.83 us

profile of v1, /device:TPU:1, one launch (start us, length us, event | category | flops | bytes accessed | tf_op | source)
XLA Modules:
  0.0 86.7 jit_solution(15831706342366433654)
XLA Ops:
  0.6 84.3 %shard_map.112.result_ref = bf16[3,32,1024]{2,1,0:T(8,128)(2,1)} custom-call(s32[1,2]{1,0:T(1,128)} %bitcast.4, bf16[512,1024]{1,0:T(8,128)(2,1)} %acts_ref.1, bf16[512,1024]{1,0:T(8,128)(2,1)} %grads_ref.1, bf16[32,1024]{1,0:T(8,128)(2,1)} %a_hbm.1, bf16[32,1024]{1,0:T(8,128)(2,1)} %b_ref.1, f32[1,32]{1,0:T(1,128)} %bitcast.5, f32[1,1024]{1,0:T(1,128)} %bitcast.3), custom_call_target="tpu_custom_call" | custom-call | flops 2147483648 | bytes 2097152 | tf_op jit(solution)/shard_map/pallas_call | solution.py:358
  84.9 1.8 %shard_map.113 = (f32[32,1024]{1,0:T(8,128)}, f32[32,1024]{1,0:T(8,128)}, f32[32,1024]{1,0:T(8,128)}) custom-call(bf16[3,32,1024]{2,1,0:T(8,128)(2,1)} %shard_map.112.result_ref, f32[32,1024]{1,0:T(8,128)} %old_act_ref.1, f32[32,1024]{1,0:T(8,128)} %old_grad_ref.1), custom_call_target="tpu_custom_call" | custom-call | tf_op jit(solution)/shard_map/pallas_call | solution.py:414

commit v2 on v1

v2 whole, which is shorter than its diff:
```python
import functools

import jax
import jax.numpy as jnp
from jax import lax
from jax.experimental import pallas as pl
from jax.experimental.pallas import tpu as pltpu
from jax.sharding import PartitionSpec as P

NX, NY, NZ, ZL = 4, 8, 8, 4
D, TOK = 1024, 512
HALF = D // 2
CHUNKS, CW = 4, 256
BF, F32 = jnp.bfloat16, jnp.float32
DX = (2, 1, 3)
DY = (4, 3, 5, 2, 6, 1, 7)
DZ = (4, 3, 5, 2, 6, 1, 7)
DZL = (2, 1, 7)
DXC = tuple((dx, dc) for dx in (2, 1, 3, 0) for dc in (1, 0) if (dx, dc) != (0, 0))
NT = (((1,), (1,)), ((), ()))


def dot(left, right, dims=(((1,), (0,)), ((), ()))):
    return lax.dot_general(left, right, dims, preferred_element_type=F32)


def column(row):
    sub = lax.broadcasted_iota(jnp.int32, (128, 128), 0)
    lane = lax.broadcasted_iota(jnp.int32, (128, 128), 1)
    return jnp.sum(jnp.where(sub == lane, row, 0.0), axis=1, keepdims=True)


def kernel(
    idx_hbm, acts_hbm, grads_hbm, a_hbm, b_hbm, aeig_hbm, geig_hbm,
    out_ref,
    idx_ref, a_ref, aeig_ref, geig_ref,
    acts_v, acts_sv, grads_v, actst, abuf, bbuf,
    tbuf, sendx1, recvx1, sendx2, recvx2, sendz, recvz, sendy, recvy,
    gbuf, recip, qbuf,
    shifted, picks, pbuf, pwide, xbuf, sfull, ssend, srecv, szsend, szrecv, sout,
    lsem, ssem, rsem,
):
    grp, dev = lax.axis_index("grp"), lax.axis_index("dev")
    y, zh = grp // 2, grp % 2
    x, zl, c = dev // 8, (dev // 2) % 4, dev % 2
    z = zh * ZL + zl

    def at(px, py, pz, pc):
        return {"grp": py * 2 + pz // ZL, "dev": px * 8 + (pz % ZL) * 2 + pc}

    def to_x(step):
        return at((x + step) % NX, y, z, c)

    def to_y(step):
        return at(x, (y + step) % NY, z, c)

    def to_z(step):
        return at(x, y, (z + step) % NZ, c)

    def to_xc(step):
        return at((x + step[0]) % NX, y, z, (c + step[1]) % 2)

    sibling = at(x, y, z, 1 - c)

    counter = [0]
    pending = []

    def send(moves, like):
        n = counter[0]
        counter[0] += 1

        def copy(src, dst, target):
            return pltpu.make_async_remote_copy(
                src_ref=src, dst_ref=dst, send_sem=ssem.at[n], recv_sem=rsem.at[n],
                device_id=target, device_id_type=pl.DeviceIdType.MESH,
            )

        for move in moves:
            copy(*move).start()
        whole = copy(like, like, sibling)
        pending.append(whole)
        return whole

    def gather(ref, targets, like):
        return send([(ref, ref, target) for target in targets], like)

    def drain():
        for copy in pending:
            copy.wait_send()
        pending.clear()

    all_x = [to_x(s) for s in DX]
    all_y = [to_y(s) for s in DY]
    all_z = [to_z(s) for s in DZ]
    all_zl = [to_z(s) for s in DZL]
    all_xc = [to_xc(s) for s in DXC]
    x_up, x_down, x_far = (x + 1) % NX, (x + 3) % NX, (x + 2) % NX

    barrier = pltpu.get_barrier_semaphore()
    partners = all_xc + all_y + all_z
    for partner in partners:
        pl.semaphore_signal(
            barrier, inc=1, device_id=partner, device_id_type=pl.DeviceIdType.MESH
        )

    my_rows = pl.ds(pl.multiple_of(c * 32, 32), 32)
    my_cols = pl.ds(pl.multiple_of(y * 128, 128), 128)

    def half(ref, side):
        return ref.at[:, pl.ds(pl.multiple_of(side * HALF, HALF), HALF)]

    def quarter(ref, side, h):
        return ref.at[:, pl.ds(pl.multiple_of(side * HALF + h * 256, 256), 256)]

    moves = [
        (acts_hbm, acts_v), (grads_hbm, grads_v.at[0]), (idx_hbm, idx_ref),
        (aeig_hbm, aeig_ref), (geig_hbm.at[:, my_cols], geig_ref), (a_hbm, a_ref),
        (b_hbm.at[pl.ds(0, 16), my_cols], pbuf.at[x, zl, c, 3]),
        (b_hbm.at[pl.ds(16, 16), my_cols], pbuf.at[x, zl, c, 4]),
    ]
    for source, whole in ((a_hbm, abuf), (b_hbm, bbuf)):
        for h in range(2):
            moves.append((quarter(source, c, h), whole.at[2 * c + h, x, zl, my_rows]))
    own = [pltpu.make_async_copy(src, dst, lsem.at[i]) for i, (src, dst) in enumerate(moves)]
    for copy in own:
        copy.start()

    own[0].wait()
    mine = acts_v[:, pl.ds(pl.multiple_of(c * HALF, HALF), HALF)]
    for k in range(2):
        for t in range(2):
            actst[256 * k:256 * k + 256, 256 * t:256 * t + 256] = (
                mine[256 * t:256 * t + 256, 256 * k:256 * k + 256].T
            )

    pl.semaphore_wait(barrier, len(partners))

    acts_sib = send([(half(acts_hbm, 1 - c), acts_sv, sibling)], acts_sv)
    grads_sib = send([(grads_hbm, grads_v.at[1], sibling)], grads_v.at[1])
    basis_sib = []
    for source, whole in ((a_hbm, abuf), (b_hbm, bbuf)):
        basis_sib.append(send(
            [
                (quarter(source, 1 - c, h), whole.at[2 * (1 - c) + h, x, zl, my_rows], sibling)
                for h in range(2)
            ],
            whole.at[pl.ds(0, 2), 0, 0, pl.ds(0, 32)],
        ))

    def term(slot, j):
        part = dot(
            actst[:, slot * TOK:slot * TOK + TOK], grads_v[slot, :, CW * j:CW * j + CW]
        )
        return part.reshape(NX, 128, CW)

    for copy in own[1:]:
        copy.wait()
    for j in range(CHUNKS):
        tbuf[j] = term(0, j)

    row = lax.broadcasted_iota(jnp.int32, (16, TOK), 0)
    col = lax.broadcasted_iota(jnp.int32, (16, TOK), 1)
    wanted = jnp.where(row == 0, idx_ref[0, 0], jnp.where(row == 1, idx_ref[0, 1], -1))
    hot = jnp.where(col == wanted, 1.0, 0.0).astype(BF)
    for i, source in enumerate((acts_v[...], grads_v[0])):
        rows = dot(hot, source)
        for s in range(2):
            for k in range(8):
                picks[i, s * 8 + k:s * 8 + k + 1, :] = rows[s:s + 1, 128 * k:128 * k + 128]
    shifted[...] = jnp.zeros((8, 128), F32)
    shifted[0:1, 0:32] = aeig_ref[...]
    eigs = pltpu.roll(shifted[...], (dev % 4) * 32, 1)[0:1, :]
    high = eigs.astype(BF).astype(F32)
    middle = (eigs - high).astype(BF).astype(F32)
    picks[2] = jnp.zeros((16, 128), F32)
    picks[2, 0:1, :] = high
    picks[2, 1:2, :] = middle
    picks[2, 2:3, :] = eigs - high - middle
    pbuf[x, zl, c, 0:3] = picks[...].astype(BF)
    pz = gather(pbuf.at[x, zl, c], all_zl, pbuf.at[0, pl.ds(0, 3), 0])

    def first(whole):
        return (
            gather(whole.at[2 * c, x, zl], all_zl, whole.at[0, 0, pl.ds(0, 3)]),
            gather(whole.at[2 * c + 1, x, zl], all_x, whole.at[0, 0, pl.ds(0, 3)]),
        )

    def second(whole, stage):
        stage[0].wait_recv()
        over_x = gather(whole.at[2 * c, x], all_x, whole.at[0, pl.ds(0, 3)])
        stage[1].wait_recv()
        over_z = gather(whole.at[2 * c + 1, :, zl], all_zl, whole.at[0, pl.ds(0, 3)])
        return over_x, over_z

    def third(whole, stage):
        for copy in stage:
            copy.wait_recv()
        mine = whole.at[pl.ds(2 * c, 2)]
        return gather(mine, [sibling], mine)

    basis_sib[0].wait_recv()
    a_first = first(abuf)
    basis_sib[1].wait_recv()
    b_first = first(bbuf)

    acts_sib.wait_recv()
    for k in range(2):
        for t in range(2):
            actst[256 * k:256 * k + 256, TOK + 256 * t:TOK + 256 * t + 256] = (
                acts_sv[256 * t:256 * t + 256, 256 * k:256 * k + 256].T
            )
    grads_sib.wait_recv()
    r1, r2 = {}, {}

    def forward(j):
        r1[j][0].wait_recv()
        sendx2[j, 0] = (tbuf[j, x_up, 0:64, :] + recvx1[j, 0, 0].astype(F32)).astype(BF)
        up = send([(sendx2.at[j, 0], recvx2.at[j, 0], to_x(1))], recvx2.at[j, 0])
        r1[j][1].wait_recv()
        sendx2[j, 1] = (tbuf[j, x_down, 64:128, :] + recvx1[j, 1, 0].astype(F32)).astype(BF)
        down = send([(sendx2.at[j, 1], recvx2.at[j, 1], to_x(3))], recvx2.at[j, 1])
        r2[j] = (up, down)

    for j in range(CHUNKS):
        tbuf[j] = tbuf[j] + term(1, j)
        sendx1[j, 0, 0] = tbuf[j, x_far, 0:64, :].astype(BF)
        sendx1[j, 0, 1] = tbuf[j, x_up, 64:128, :].astype(BF)
        sendx1[j, 1, 0] = tbuf[j, x_far, 64:128, :].astype(BF)
        sendx1[j, 1, 1] = tbuf[j, x_down, 0:64, :].astype(BF)
        r1[j] = [
            send([(sendx1.at[j, i], recvx1.at[j, i], to_x(s))], recvx1.at[j, i])
            for i, s in enumerate((1, 3))
        ]
        if j > 1:
            forward(j - 2)
    pz.wait_recv()
    px = gather(pbuf.at[x, :, c], all_x, pbuf.at[pl.ds(0, 3), :, 0])
    forward(CHUNKS - 2)
    forward(CHUNKS - 1)
    a_second = second(abuf, a_first)

    rz, ry = {}, {}

    def sum_x(j):
        r2[j][0].wait_recv()
        r2[j][1].wait_recv()
        top = tbuf[j, x, 0:64, :] + recvx1[j, 1, 1].astype(F32) + recvx2[j, 0].astype(F32)
        low = tbuf[j, x, 64:128, :] + recvx1[j, 0, 1].astype(F32) + recvx2[j, 1].astype(F32)
        sendz[j, 0:4] = top.astype(BF).reshape(4, 16, CW)
        sendz[j, 4:8] = low.astype(BF).reshape(4, 16, CW)
        rz[j] = send(
            [(sendz.at[j, (z + s) % NZ], recvz.at[j, i], to_z(s)) for i, s in enumerate(DZ)],
            recvz.at[j],
        )

    def sum_z(j):
        rz[j].wait_recv()
        total = sendz[j, z].astype(F32)
        for i in range(len(DZ)):
            total = total + recvz[j, i].astype(F32)
        sendy[j] = total.astype(BF)
        ry[j] = send(
            [(sendy.at[j], recvy.at[j, i], to_y(s)) for i, s in enumerate(DY)], recvy.at[j]
        )

    sum_x(0)
    for j in range(1, CHUNKS):
        sum_x(j)
        sum_z(j - 1)
    px.wait_recv()
    psib = gather(pbuf.at[:, :, c], [sibling], pbuf.at[:, :, c])
    sum_z(CHUNKS - 1)
    b_second = second(bbuf, b_first)

    psib.wait_recv()
    for i in range(2):
        pwide[...] = pbuf[:, :, :, i].reshape(2 * NX * ZL * 16, 128).astype(F32)
        for k in range(8):
            part = jnp.concatenate(
                [pwide[pl.ds(s * 8 + k, 2 * NX * ZL, stride=16), :] for s in range(2)], axis=0
            )
            xbuf[k] = part.astype(BF)
        wide = jnp.concatenate([xbuf[k] for k in range(8)], axis=1)
        sfull[...] = dot(xbuf[dev // 4], wide, (((0,), (0,)), ((), ())))
        rows = sfull[pl.ds(pl.multiple_of((dev % 4) * 32, 32), 32), :]
        for k in range(8):
            ssend[k, i] = rows[:, 128 * k:128 * k + 128].astype(BF)
    sy = send([(ssend.at[(y + s) % NY], srecv.at[i], to_y(s)) for i, s in enumerate(DY)], srecv)

    high_parts, low_parts = [], []
    for j in range(CHUNKS):
        ry[j].wait_recv()
        total = sendy[j].astype(F32)
        for i in range(len(DY)):
            total = total + recvy[j, i].astype(F32)
        high_parts.append(total.astype(BF))
        low_parts.append((total - total.astype(BF).astype(F32)).astype(BF))
    columns = pbuf[:, :, :, 3:5].reshape(D, 128)
    product = dot(
        jnp.concatenate(
            [jnp.concatenate(high_parts, axis=1), jnp.concatenate(low_parts, axis=1)], axis=0
        ),
        columns,
    )
    gbuf[c * NX + x, z] = (product[0:16] + product[16:32]).astype(BF)
    mine = gbuf.at[c * NX + x]
    gz = gather(mine.at[z], all_z, gbuf.at[0, pl.ds(0, 7)])

    geig = column(geig_ref[...])
    for m in range(8):
        block = pbuf[m // 2, 2 * (m % 2):2 * (m % 2) + 2, :, 2].astype(F32)
        block = block[0, 0] + block[0, 1] + block[1, 0] + block[1, 1]
        eig_row = block[0:1] + block[1:2] + block[2:3]
        recip[:, 128 * m:128 * m + 128] = 1.0 / (geig * eig_row + 0.1)

    gz.wait_recv()
    gxc = gather(mine, all_xc, gbuf.at[pl.ds(0, 7)])
    a_third = third(abuf, a_second)

    sy.wait_recv()
    stat = ssend[y].astype(F32)
    for i in range(len(DY)):
        stat = stat + srecv[i].astype(F32)
    szsend[...] = stat
    sz = send([(szsend, szrecv, to_z(4))], szrecv)

    gxc.wait_recv()
    turned = gbuf[...].reshape(D, 128).T
    a_third.wait_recv()
    total = jnp.zeros((32, 128), F32)
    for q in range(4):
        cols = slice(256 * q, 256 * q + 256)
        scaled = (dot(turned, abuf[q].reshape(D, 256)) * recip[:, cols]).astype(BF)
        total = total + dot(a_ref[:, cols], scaled, NT)
    qbuf[y] = total.astype(BF)
    qy = gather(qbuf.at[y], all_y, qbuf.at[pl.ds(0, 7)])
    b_third = third(bbuf, b_second)

    sz.wait_recv()
    sout[y] = (szsend[...] + szrecv[...]).astype(BF)
    so = gather(sout.at[y], all_y, sout.at[pl.ds(0, 7)])
    drain()

    qy.wait_recv()
    left = jnp.concatenate([qbuf[k] for k in range(8)], axis=1)
    b_third.wait_recv()
    total = dot(left[:, 0:256], bbuf[0].reshape(D, 256), NT)
    for q in range(1, 4):
        total = total + dot(left[:, 256 * q:256 * q + 256], bbuf[q].reshape(D, 256), NT)
    out_ref[0] = total
    so.wait_recv()
    for i in range(2):
        for k in range(8):
            out_ref[1 + i, :, 128 * k:128 * k + 128] = sout[k, i].astype(F32)


def finish(result_ref, old_act_ref, old_grad_ref, pre_ref, act_ref, grad_ref, *, act_scale, grad_scale):
    pre_ref[...] = result_ref[0]
    act_ref[...] = 0.75 * old_act_ref[...] + act_scale * result_ref[1]
    grad_ref[...] = 0.75 * old_grad_ref[...] + grad_scale * result_ref[2]


def local(
    acts,
    out_grads,
    old_act_factor,
    old_grad_factor,
    act_basis,
    grad_basis,
    act_eigs,
    grad_eigs,
    sample_index,
):
    vmem = pl.BlockSpec(memory_space=pltpu.VMEM)
    hbm = pl.BlockSpec(memory_space=pl.ANY)
    copies = 72
    result = pl.pallas_call(
        kernel,
        out_shape=jax.ShapeDtypeStruct((3, 32, D), F32),
        in_specs=[hbm] * 7,
        out_specs=vmem,
        scratch_shapes=[
            pltpu.SMEM((1, 2), jnp.int32),
            pltpu.VMEM((32, D), BF),
            pltpu.VMEM((1, 32), F32),
            pltpu.VMEM((1, 128), F32),
            pltpu.VMEM((TOK, D), BF),
            pltpu.VMEM((TOK, HALF), BF),
            pltpu.VMEM((2, TOK, D), BF),
            pltpu.VMEM((HALF, 2 * TOK), BF),
            pltpu.VMEM((4, NX, ZL, 64, 256), BF),
            pltpu.VMEM((4, NX, ZL, 64, 256), BF),
            pltpu.VMEM((CHUNKS, NX, 128, CW), F32),
            pltpu.VMEM((CHUNKS, 2, 2, 64, CW), BF),
            pltpu.VMEM((CHUNKS, 2, 2, 64, CW), BF),
            pltpu.VMEM((CHUNKS, 2, 64, CW), BF),
            pltpu.VMEM((CHUNKS, 2, 64, CW), BF),
            pltpu.VMEM((CHUNKS, NZ, 16, CW), BF),
            pltpu.VMEM((CHUNKS, 7, 16, CW), BF),
            pltpu.VMEM((CHUNKS, 16, CW), BF),
            pltpu.VMEM((CHUNKS, 7, 16, CW), BF),
            pltpu.VMEM((2 * NX, NZ, 16, 128), BF),
            pltpu.VMEM((128, D), F32),
            pltpu.VMEM((NY, 32, 128), BF),
            pltpu.VMEM((8, 128), F32),
            pltpu.VMEM((3, 16, 128), F32),
            pltpu.VMEM((NX, ZL, 2, 5, 16, 128), BF),
            pltpu.VMEM((2 * NX * ZL * 16, 128), F32),
            pltpu.VMEM((8, 64, 128), BF),
            pltpu.VMEM((128, D), F32),
            pltpu.VMEM((NY, 2, 32, 128), BF),
            pltpu.VMEM((7, 2, 32, 128), BF),
            pltpu.VMEM((2, 32, 128), F32),
            pltpu.VMEM((2, 32, 128), F32),
            pltpu.VMEM((NY, 2, 32, 128), BF),
            pltpu.SemaphoreType.DMA((12,)),
            pltpu.SemaphoreType.DMA((copies,)),
            pltpu.SemaphoreType.DMA((copies,)),
        ],
        compiler_params=pltpu.CompilerParams(
            collective_id=0, has_side_effects=True, vmem_limit_bytes=63 * 1024 * 1024
        ),
        cost_estimate=pl.CostEstimate(
            flops=4 * TOK * D * D, bytes_accessed=4 * TOK * D, transcendentals=0
        ),
    )(
        sample_index.reshape(1, 2), acts, out_grads, act_basis, grad_basis,
        act_eigs.reshape(1, 32), grad_eigs.reshape(1, D),
    )
    device_count = lax.axis_size("grp") * lax.axis_size("dev")
    total_samples = device_count * sample_index.shape[0]
    total_tokens = device_count * acts.shape[0]
    return pl.pallas_call(
        functools.partial(
            finish,
            act_scale=0.25 / total_samples,
            grad_scale=0.25 * total_tokens / total_samples,
        ),
        out_shape=(jax.ShapeDtypeStruct((32, D), F32),) * 3,
        in_specs=[vmem] * 3,
        out_specs=(vmem,) * 3,
    )(result, old_act_factor, old_grad_factor)


def solution(mesh):
    return jax.shard_map(
        local,
        mesh=mesh,
        in_specs=(
            P(("grp", "dev"), None),
            P(("grp", "dev"), None),
            P("dev", None),
            P("dev", None),
            P("dev", None),
            P("dev", None),
            P("dev"),
            P(),
            P(("grp", "dev")),
        ),
        out_specs=(P("dev", None), P("dev", None), P("dev", None)),
        check_vma=False,
    )
```

time: 86.9 us -> 76.9 us (0.88)
  Pallas kernels: 86.1 us -> 76.1 us
    pallas_call x1, Pallas kernels: 84.3 us -> 74.2 us  [local(): pl.pallas_call(kernel, out_shape=jax.ShapeDtypeStruct((3, 32, D), F32), i...]
where the time goes in v2:
time: 76.9 us; the launch traced here: 76.7 us
  Pallas kernels  76.1 us (99%)
    pallas_call x1, Pallas kernels, local(): pl.pallas_call(kernel, out_shape=jax.ShapeDtypeStruct((3, 32, D), F32), i...  74.2 us
    pallas_call x1, Pallas kernels, local(): pl.pallas_call(functools.partial(finish, act_scale=0.25 / total_samples,...  1.86 us

profile of v2, /device:TPU:1, one launch (start us, length us, event | category | flops | bytes accessed | tf_op | source)
XLA Modules:
  0.0 76.7 jit_solution(9573494242781146560)
XLA Ops:
  0.6 74.2 %shard_map.112.result_ref = f32[3,32,1024]{2,1,0:T(8,128)} custom-call(s32[1,2]{1,0:T(1,128)} %bitcast.4, bf16[512,1024]{1,0:T(8,128)(2,1)} %acts_hbm.1, bf16[512,1024]{1,0:T(8,128)(2,1)} %grads_hbm.1, bf16[32,1024]{1,0:T(8,128)(2,1)} %a_hbm.1, bf16[32,1024]{1,0:T(8,128)(2,1)} %b_hbm.1, f32[1,32]{1,0:T(1,128)} %bitcast.5, f32[1,1024]{1,0:T(1,128)} %bitcast.3), custom_call_target="tpu_custom_call" | custom-call | flops 2147483648 | bytes 2097152 | tf_op jit(solution)/shard_map/pallas_call | solution.py:377
  74.9 1.9 %shard_map.113 = (f32[32,1024]{1,0:T(8,128)}, f32[32,1024]{1,0:T(8,128)}, f32[32,1024]{1,0:T(8,128)}) custom-call(f32[3,32,1024]{2,1,0:T(8,128)} %shard_map.112.result_ref, f32[32,1024]{1,0:T(8,128)} %old_act_ref.1, f32[32,1024]{1,0:T(8,128)} %old_grad_ref.1), custom_call_target="tpu_custom_call" | custom-call | tf_op jit(solution)/shard_map/pallas_call | solution.py:433

commit v3 on v2

--- a/solution.py
+++ b/solution.py
@@ -37,7 +37,7 @@
     acts_v, acts_sv, grads_v, actst, abuf, bbuf,
     tbuf, sendx1, recvx1, sendx2, recvx2, sendz, recvz, sendy, recvy,
     gbuf, recip, qbuf,
-    shifted, picks, pbuf, pwide, xbuf, sfull, ssend, srecv, szsend, szrecv, sout,
+    shifted, parts, ebuf, picks, pbuf, pwide, xbuf, sfull, ssend, srecv, szsend, szrecv, sout,
     lsem, ssem, rsem,
 ):
     grp, dev = lax.axis_index("grp"), lax.axis_index("dev")
@@ -113,10 +113,11 @@
         return ref.at[:, pl.ds(pl.multiple_of(side * HALF + h * 256, 256), 256)]
 
     moves = [
+        (aeig_hbm, aeig_ref),
+        (b_hbm.at[pl.ds(0, 16), my_cols], ebuf.at[x, zl, c, 1]),
+        (b_hbm.at[pl.ds(16, 16), my_cols], ebuf.at[x, zl, c, 2]),
         (acts_hbm, acts_v), (grads_hbm, grads_v.at[0]), (idx_hbm, idx_ref),
-        (aeig_hbm, aeig_ref), (geig_hbm.at[:, my_cols], geig_ref), (a_hbm, a_ref),
-        (b_hbm.at[pl.ds(0, 16), my_cols], pbuf.at[x, zl, c, 3]),
-        (b_hbm.at[pl.ds(16, 16), my_cols], pbuf.at[x, zl, c, 4]),
+        (geig_hbm.at[:, my_cols], geig_ref), (a_hbm, a_ref),
     ]
     for source, whole in ((a_hbm, abuf), (b_hbm, bbuf)):
         for h in range(2):
@@ -126,17 +127,21 @@
         copy.start()
 
     own[0].wait()
-    mine = acts_v[:, pl.ds(pl.multiple_of(c * HALF, HALF), HALF)]
-    for k in range(2):
-        for t in range(2):
-            actst[256 * k:256 * k + 256, 256 * t:256 * t + 256] = (
-                mine[256 * t:256 * t + 256, 256 * k:256 * k + 256].T
-            )
+    shifted[...] = jnp.zeros((8, 128), F32)
+    shifted[0:1, 0:32] = aeig_ref[...]
+    eigs = pltpu.roll(shifted[...], (dev % 4) * 32, 1)[0:1, :]
+    high = eigs.astype(BF).astype(F32)
+    middle = (eigs - high).astype(BF).astype(F32)
+    parts[...] = jnp.zeros((16, 128), F32)
+    parts[0:1, :] = high
+    parts[1:2, :] = middle
+    parts[2:3, :] = eigs - high - middle
+    ebuf[x, zl, c, 0] = parts[...].astype(BF)
+    for copy in own[1:3]:
+        copy.wait()
 
     pl.semaphore_wait(barrier, len(partners))
 
-    acts_sib = send([(half(acts_hbm, 1 - c), acts_sv, sibling)], acts_sv)
-    grads_sib = send([(grads_hbm, grads_v.at[1], sibling)], grads_v.at[1])
     basis_sib = []
     for source, whole in ((a_hbm, abuf), (b_hbm, bbuf)):
         basis_sib.append(send(
@@ -147,37 +152,28 @@
             whole.at[pl.ds(0, 2), 0, 0, pl.ds(0, 32)],
         ))
 
+    acts_sib = send([(half(acts_hbm, 1 - c), acts_sv, sibling)], acts_sv)
+    grads_sib = send([(grads_hbm, grads_v.at[1], sibling)], grads_v.at[1])
+    ez = gather(ebuf.at[x, zl, c], all_zl, ebuf.at[0, pl.ds(0, 3), 0])
+
+    own[3].wait()
+    mine = acts_v[:, pl.ds(pl.multiple_of(c * HALF, HALF), HALF)]
+    for k in range(2):
+        for t in range(2):
+            actst[256 * k:256 * k + 256, 256 * t:256 * t + 256] = (
+                mine[256 * t:256 * t + 256, 256 * k:256 * k + 256].T
+            )
+
     def term(slot, j):
         part = dot(
             actst[:, slot * TOK:slot * TOK + TOK], grads_v[slot, :, CW * j:CW * j + CW]
         )
         return part.reshape(NX, 128, CW)
 
-    for copy in own[1:]:
+    for copy in own[4:]:
         copy.wait()
     for j in range(CHUNKS):
         tbuf[j] = term(0, j)
-
-    row = lax.broadcasted_iota(jnp.int32, (16, TOK), 0)
-    col = lax.broadcasted_iota(jnp.int32, (16, TOK), 1)
-    wanted = jnp.where(row == 0, idx_ref[0, 0], jnp.where(row == 1, idx_ref[0, 1], -1))
-    hot = jnp.where(col == wanted, 1.0, 0.0).astype(BF)
-    for i, source in enumerate((acts_v[...], grads_v[0])):
-        rows = dot(hot, source)
-        for s in range(2):
-            for k in range(8):
-                picks[i, s * 8 + k:s * 8 + k + 1, :] = rows[s:s + 1, 128 * k:128 * k + 128]
-    shifted[...] = jnp.zeros((8, 128), F32)
-    shifted[0:1, 0:32] = aeig_ref[...]
-    eigs = pltpu.roll(shifted[...], (dev % 4) * 32, 1)[0:1, :]
-    high = eigs.astype(BF).astype(F32)
-    middle = (eigs - high).astype(BF).astype(F32)
-    picks[2] = jnp.zeros((16, 128), F32)
-    picks[2, 0:1, :] = high
-    picks[2, 1:2, :] = middle
-    picks[2, 2:3, :] = eigs - high - middle
-    pbuf[x, zl, c, 0:3] = picks[...].astype(BF)
-    pz = gather(pbuf.at[x, zl, c], all_zl, pbuf.at[0, pl.ds(0, 3), 0])
 
     def first(whole):
         return (
@@ -185,12 +181,13 @@
             gather(whole.at[2 * c + 1, x, zl], all_x, whole.at[0, 0, pl.ds(0, 3)]),
         )
 
-    def second(whole, stage):
+    def second_x(whole, stage):
         stage[0].wait_recv()
-        over_x = gather(whole.at[2 * c, x], all_x, whole.at[0, pl.ds(0, 3)])
+        return gather(whole.at[2 * c, x], all_x, whole.at[0, pl.ds(0, 3)])
+
+    def second_z(whole, stage):
         stage[1].wait_recv()
-        over_z = gather(whole.at[2 * c + 1, :, zl], all_zl, whole.at[0, pl.ds(0, 3)])
-        return over_x, over_z
+        return gather(whole.at[2 * c + 1, :, zl], all_zl, whole.at[0, pl.ds(0, 3)])
 
     def third(whole, stage):
         for copy in stage:
@@ -202,6 +199,8 @@
     a_first = first(abuf)
     basis_sib[1].wait_recv()
     b_first = first(bbuf)
+    ez.wait_recv()
+    ex = gather(ebuf.at[x, :, c], all_x, ebuf.at[pl.ds(0, 3), :, 0])
 
     acts_sib.wait_recv()
     for k in range(2):
@@ -231,13 +230,27 @@
             send([(sendx1.at[j, i], recvx1.at[j, i], to_x(s))], recvx1.at[j, i])
             for i, s in enumerate((1, 3))
         ]
-        if j > 1:
-            forward(j - 2)
+    a_over_z = second_z(abuf, a_first)
+
+    row = lax.broadcasted_iota(jnp.int32, (16, TOK), 0)
+    col = lax.broadcasted_iota(jnp.int32, (16, TOK), 1)
+    wanted = jnp.where(row == 0, idx_ref[0, 0], jnp.where(row == 1, idx_ref[0, 1], -1))
+    hot = jnp.where(col == wanted, 1.0, 0.0).astype(BF)
+    for i, source in enumerate((acts_v[...], grads_v[0])):
+        rows = dot(hot, source)
+        for s in range(2):
+            for k in range(8):
+                picks[i, s * 8 + k:s * 8 + k + 1, :] = rows[s:s + 1, 128 * k:128 * k + 128]
+    pbuf[x, zl, c] = picks[...].astype(BF)
+    pz = gather(pbuf.at[x, zl, c], all_zl, pbuf.at[0, pl.ds(0, 3), 0])
+
+    for j in range(CHUNKS):
+        forward(j)
+    ex.wait_recv()
+    esib = gather(ebuf.at[:, :, c], [sibling], ebuf.at[:, :, c])
     pz.wait_recv()
     px = gather(pbuf.at[x, :, c], all_x, pbuf.at[pl.ds(0, 3), :, 0])
-    forward(CHUNKS - 2)
-    forward(CHUNKS - 1)
-    a_second = second(abuf, a_first)
+    a_over_x = second_x(abuf, a_first)
 
     rz, ry = {}, {}
 
@@ -267,10 +280,10 @@
     for j in range(1, CHUNKS):
         sum_x(j)
         sum_z(j - 1)
+    sum_z(CHUNKS - 1)
     px.wait_recv()
     psib = gather(pbuf.at[:, :, c], [sibling], pbuf.at[:, :, c])
-    sum_z(CHUNKS - 1)
-    b_second = second(bbuf, b_first)
+    b_over_x = second_x(bbuf, b_first)
 
     psib.wait_recv()
     for i in range(2):
@@ -295,7 +308,8 @@
             total = total + recvy[j, i].astype(F32)
         high_parts.append(total.astype(BF))
         low_parts.append((total - total.astype(BF).astype(F32)).astype(BF))
-    columns = pbuf[:, :, :, 3:5].reshape(D, 128)
+    esib.wait_recv()
+    columns = ebuf[:, :, :, 1:3].reshape(D, 128)
     product = dot(
         jnp.concatenate(
             [jnp.concatenate(high_parts, axis=1), jnp.concatenate(low_parts, axis=1)], axis=0
@@ -305,17 +319,18 @@
     gbuf[c * NX + x, z] = (product[0:16] + product[16:32]).astype(BF)
     mine = gbuf.at[c * NX + x]
     gz = gather(mine.at[z], all_z, gbuf.at[0, pl.ds(0, 7)])
+    b_over_z = second_z(bbuf, b_first)
 
     geig = column(geig_ref[...])
     for m in range(8):
-        block = pbuf[m // 2, 2 * (m % 2):2 * (m % 2) + 2, :, 2].astype(F32)
+        block = ebuf[m // 2, 2 * (m % 2):2 * (m % 2) + 2, :, 0].astype(F32)
         block = block[0, 0] + block[0, 1] + block[1, 0] + block[1, 1]
         eig_row = block[0:1] + block[1:2] + block[2:3]
         recip[:, 128 * m:128 * m + 128] = 1.0 / (geig * eig_row + 0.1)
 
     gz.wait_recv()
     gxc = gather(mine, all_xc, gbuf.at[pl.ds(0, 7)])
-    a_third = third(abuf, a_second)
+    a_third = third(abuf, (a_over_x, a_over_z))
 
     sy.wait_recv()
     stat = ssend[y].astype(F32)
@@ -334,7 +349,7 @@
         total = total + dot(a_ref[:, cols], scaled, NT)
     qbuf[y] = total.astype(BF)
     qy = gather(qbuf.at[y], all_y, qbuf.at[pl.ds(0, 7)])
-    b_third = third(bbuf, b_second)
+    b_third = third(bbuf, (b_over_x, b_over_z))
 
     sz.wait_recv()
     sout[y] = (szsend[...] + szrecv[...]).astype(BF)
@@ -403,8 +418,10 @@
             pltpu.VMEM((128, D), F32),
             pltpu.VMEM((NY, 32, 128), BF),
             pltpu.VMEM((8, 128), F32),
-            pltpu.VMEM((3, 16, 128), F32),
-            pltpu.VMEM((NX, ZL, 2, 5, 16, 128), BF),
+            pltpu.VMEM((16, 128), F32),
+            pltpu.VMEM((NX, ZL, 2, 3, 16, 128), BF),
+            pltpu.VMEM((2, 16, 128), F32),
+            pltpu.VMEM((NX, ZL, 2, 2, 16, 128), BF),
             pltpu.VMEM((2 * NX * ZL * 16, 128), F32),
             pltpu.VMEM((8, 64, 128), BF),
             pltpu.VMEM((128, D), F32),

time: 76.9 us -> 69.3 us (0.901)
  Pallas kernels: 76.1 us -> 68.5 us
    pallas_call x1, Pallas kernels: 74.2 us -> 66.7 us  [local(): pl.pallas_call(kernel, out_shape=jax.ShapeDtypeStruct((3, 32, D), F32), i...]
where the time goes in v3:
time: 69.3 us; the launch traced here: 69.2 us
  Pallas kernels  68.5 us (99%)
    pallas_call x1, Pallas kernels, local(): pl.pallas_call(kernel, out_shape=jax.ShapeDtypeStruct((3, 32, D), F32), i...  66.7 us
    pallas_call x1, Pallas kernels, local(): pl.pallas_call(functools.partial(finish, act_scale=0.25 / total_samples,...  1.86 us

profile of v3, /device:TPU:1, one launch (start us, length us, event | category | flops | bytes accessed | tf_op | source)
XLA Modules:
  0.0 69.2 jit_solution(17066879010438447256)
XLA Ops:
  0.6 66.7 %shard_map.112.result_ref = f32[3,32,1024]{2,1,0:T(8,128)} custom-call(s32[1,2]{1,0:T(1,128)} %bitcast.4, bf16[512,1024]{1,0:T(8,128)(2,1)} %acts_hbm.1, bf16[512,1024]{1,0:T(8,128)(2,1)} %grads_hbm.1, bf16[32,1024]{1,0:T(8,128)(2,1)} %a_hbm.1, bf16[32,1024]{1,0:T(8,128)(2,1)} %b_hbm.1, f32[1,32]{1,0:T(1,128)} %bitcast.5, f32[1,1024]{1,0:T(1,128)} %bitcast.3), custom_call_target="tpu_custom_call" | custom-call | flops 2147483648 | bytes 2097152 | tf_op jit(solution)/shard_map/pallas_call | solution.py:392
  67.3 1.9 %shard_map.113 = (f32[32,1024]{1,0:T(8,128)}, f32[32,1024]{1,0:T(8,128)}, f32[32,1024]{1,0:T(8,128)}) custom-call(f32[3,32,1024]{2,1,0:T(8,128)} %shard_map.112.result_ref, f32[32,1024]{1,0:T(8,128)} %old_act_ref.1, f32[32,1024]{1,0:T(8,128)} %old_grad_ref.1), custom_call_target="tpu_custom_call" | custom-call | tf_op jit(solution)/shard_map/pallas_call | solution.py:450

commit v4 on v3

--- a/solution.py
+++ b/solution.py
@@ -95,6 +95,7 @@
     all_zl = [to_z(s) for s in DZL]
     all_xc = [to_xc(s) for s in DXC]
     x_up, x_down, x_far = (x + 1) % NX, (x + 3) % NX, (x + 2) % NX
+    zl_up, zl_down = (zl + 1) % ZL, (zl + 3) % ZL
 
     barrier = pltpu.get_barrier_semaphore()
     partners = all_xc + all_y + all_z
@@ -123,6 +124,23 @@
         for h in range(2):
             moves.append((quarter(source, c, h), whole.at[2 * c + h, x, zl, my_rows]))
     own = [pltpu.make_async_copy(src, dst, lsem.at[i]) for i, (src, dst) in enumerate(moves)]
+    pl.semaphore_wait(barrier, len(partners))
+
+    basis_sib = []
+    for source, whole in ((a_hbm, abuf), (b_hbm, bbuf)):
+        basis_sib.append(send(
+            [
+                (quarter(source, 1 - c, h), whole.at[2 * (1 - c) + h, x, zl, my_rows], sibling)
+                for h in range(2)
+            ],
+            whole.at[pl.ds(0, 2), 0, 0, pl.ds(0, 32)],
+        ))
+
+    acts_sib = send([(half(acts_hbm, 1 - c), acts_sv, sibling)], acts_sv)
+    grads_sib = []
+    for j in range(CHUNKS):
+        piece = grads_v.at[1, :, pl.ds(CW * j, CW)]
+        grads_sib.append(send([(grads_hbm.at[:, pl.ds(CW * j, CW)], piece, sibling)], piece))
     for copy in own:
         copy.start()
 
@@ -139,21 +157,6 @@
     ebuf[x, zl, c, 0] = parts[...].astype(BF)
     for copy in own[1:3]:
         copy.wait()
-
-    pl.semaphore_wait(barrier, len(partners))
-
-    basis_sib = []
-    for source, whole in ((a_hbm, abuf), (b_hbm, bbuf)):
-        basis_sib.append(send(
-            [
-                (quarter(source, 1 - c, h), whole.at[2 * (1 - c) + h, x, zl, my_rows], sibling)
-                for h in range(2)
-            ],
-            whole.at[pl.ds(0, 2), 0, 0, pl.ds(0, 32)],
-        ))
-
-    acts_sib = send([(half(acts_hbm, 1 - c), acts_sv, sibling)], acts_sv)
-    grads_sib = send([(grads_hbm, grads_v.at[1], sibling)], grads_v.at[1])
     ez = gather(ebuf.at[x, zl, c], all_zl, ebuf.at[0, pl.ds(0, 3), 0])
 
     own[3].wait()
@@ -164,51 +167,71 @@
                 mine[256 * t:256 * t + 256, 256 * k:256 * k + 256].T
             )
 
+    def first(whole):
+        return (
+            gather(whole.at[2 * c, x, zl], all_zl, whole.at[0, 0, pl.ds(0, 3)]),
+            gather(whole.at[2 * c + 1, x, zl], all_x, whole.at[0, 0, pl.ds(0, 3)]),
+        )
+
+    def near_x(whole):
+        mine = whole.at[2 * c, x]
+        return [send([(mine, mine, to_x(s))], mine) for s in (1, 3)]
+
+    def near_z(whole):
+        mine = whole.at[2 * c + 1, :, zl]
+        return [send([(mine, mine, to_z(s))], mine) for s in (1, 7)]
+
+    def onward(whole, over_x, over_z):
+        out = []
+        for block, target, copy in (
+            (whole.at[2 * c, x_down, pl.ds(0, 2)], to_x(1), over_x[0]),
+            (whole.at[2 * c, x_up, pl.ds(2, 2)], to_x(3), over_x[1]),
+            (whole.at[2 * c + 1, pl.ds(0, 2), zl_down], to_z(1), over_z[0]),
+            (whole.at[2 * c + 1, pl.ds(2, 2), zl_up], to_z(7), over_z[1]),
+        ):
+            copy.wait_recv()
+            out.append(send([(block, block, target)], block))
+        return out
+
+    def third(whole, stage):
+        for copy in stage:
+            copy.wait_recv()
+        mine = whole.at[pl.ds(2 * c, 2)]
+        return gather(mine, [sibling], mine)
+
+    for copy in own[4:]:
+        copy.wait()
+    basis_sib[0].wait_recv()
+    a_first = first(abuf)
+
     def term(slot, j):
         part = dot(
             actst[:, slot * TOK:slot * TOK + TOK], grads_v[slot, :, CW * j:CW * j + CW]
         )
         return part.reshape(NX, 128, CW)
 
-    for copy in own[4:]:
-        copy.wait()
     for j in range(CHUNKS):
         tbuf[j] = term(0, j)
-
-    def first(whole):
-        return (
-            gather(whole.at[2 * c, x, zl], all_zl, whole.at[0, 0, pl.ds(0, 3)]),
-            gather(whole.at[2 * c + 1, x, zl], all_x, whole.at[0, 0, pl.ds(0, 3)]),
-        )
-
-    def second_x(whole, stage):
-        stage[0].wait_recv()
-        return gather(whole.at[2 * c, x], all_x, whole.at[0, pl.ds(0, 3)])
-
-    def second_z(whole, stage):
-        stage[1].wait_recv()
-        return gather(whole.at[2 * c + 1, :, zl], all_zl, whole.at[0, pl.ds(0, 3)])
-
-    def third(whole, stage):
-        for copy in stage:
-            copy.wait_recv()
-        mine = whole.at[pl.ds(2 * c, 2)]
-        return gather(mine, [sibling], mine)
-
-    basis_sib[0].wait_recv()
-    a_first = first(abuf)
-    basis_sib[1].wait_recv()
-    b_first = first(bbuf)
-    ez.wait_recv()
-    ex = gather(ebuf.at[x, :, c], all_x, ebuf.at[pl.ds(0, 3), :, 0])
-
     acts_sib.wait_recv()
     for k in range(2):
         for t in range(2):
             actst[256 * k:256 * k + 256, TOK + 256 * t:TOK + 256 * t + 256] = (
                 acts_sv[256 * t:256 * t + 256, 256 * k:256 * k + 256].T
             )
-    grads_sib.wait_recv()
+
+    def pick():
+        row = lax.broadcasted_iota(jnp.int32, (16, TOK), 0)
+        col = lax.broadcasted_iota(jnp.int32, (16, TOK), 1)
+        wanted = jnp.where(row == 0, idx_ref[0, 0], jnp.where(row == 1, idx_ref[0, 1], -1))
+        hot = jnp.where(col == wanted, 1.0, 0.0).astype(BF)
+        for i, source in enumerate((acts_v[...], grads_v[0])):
+            rows = dot(hot, source)
+            for s in range(2):
+                for k in range(8):
+                    picks[i, s * 8 + k:s * 8 + k + 1, :] = rows[s:s + 1, 128 * k:128 * k + 128]
+        pbuf[x, zl, c] = picks[...].astype(BF)
+        return gather(pbuf.at[x, zl, c], all_zl, pbuf.at[0, pl.ds(0, 3), 0])
+
     r1, r2 = {}, {}
 
     def forward(j):
@@ -221,6 +244,7 @@
         r2[j] = (up, down)
 
     for j in range(CHUNKS):
+        grads_sib[j].wait_recv()
         tbuf[j] = tbuf[j] + term(1, j)
         sendx1[j, 0, 0] = tbuf[j, x_far, 0:64, :].astype(BF)
         sendx1[j, 0, 1] = tbuf[j, x_up, 64:128, :].astype(BF)
@@ -230,27 +254,22 @@
             send([(sendx1.at[j, i], recvx1.at[j, i], to_x(s))], recvx1.at[j, i])
             for i, s in enumerate((1, 3))
         ]
-    a_over_z = second_z(abuf, a_first)
-
-    row = lax.broadcasted_iota(jnp.int32, (16, TOK), 0)
-    col = lax.broadcasted_iota(jnp.int32, (16, TOK), 1)
-    wanted = jnp.where(row == 0, idx_ref[0, 0], jnp.where(row == 1, idx_ref[0, 1], -1))
-    hot = jnp.where(col == wanted, 1.0, 0.0).astype(BF)
-    for i, source in enumerate((acts_v[...], grads_v[0])):
-        rows = dot(hot, source)
-        for s in range(2):
-            for k in range(8):
-                picks[i, s * 8 + k:s * 8 + k + 1, :] = rows[s:s + 1, 128 * k:128 * k + 128]
-    pbuf[x, zl, c] = picks[...].astype(BF)
-    pz = gather(pbuf.at[x, zl, c], all_zl, pbuf.at[0, pl.ds(0, 3), 0])
-
-    for j in range(CHUNKS):
-        forward(j)
-    ex.wait_recv()
-    esib = gather(ebuf.at[:, :, c], [sibling], ebuf.at[:, :, c])
+        if j == 2:
+            a_first[1].wait_recv()
+            a_over_z = near_z(abuf)
+            pz = pick()
+        if j > 1:
+            forward(j - 2)
+    forward(CHUNKS - 2)
+    forward(CHUNKS - 1)
+    ez.wait_recv()
+    ex = gather(ebuf.at[x, :, c], all_x, ebuf.at[pl.ds(0, 3), :, 0])
     pz.wait_recv()
     px = gather(pbuf.at[x, :, c], all_x, pbuf.at[pl.ds(0, 3), :, 0])
-    a_over_x = second_x(abuf, a_first)
+    a_first[0].wait_recv()
+    a_over_x = near_x(abuf)
+    basis_sib[1].wait_recv()
+    b_first = first(bbuf)
 
     rz, ry = {}, {}
 
@@ -277,13 +296,48 @@
         )
 
     sum_x(0)
-    for j in range(1, CHUNKS):
-        sum_x(j)
-        sum_z(j - 1)
-    sum_z(CHUNKS - 1)
+    sum_x(1)
+    sum_z(0)
+    sum_x(2)
+    sum_z(1)
+    sum_x(3)
+    sum_z(2)
+    ex.wait_recv()
+    esib = gather(ebuf.at[:, :, c], [sibling], ebuf.at[:, :, c])
+    sum_z(3)
+    for copy in b_first:
+        copy.wait_recv()
+    a_onward = onward(abuf, a_over_x, a_over_z)
+    b_over_x, b_over_z = near_x(bbuf), near_z(bbuf)
     px.wait_recv()
     psib = gather(pbuf.at[:, :, c], [sibling], pbuf.at[:, :, c])
-    b_over_x = second_x(bbuf, b_first)
+
+    esib.wait_recv()
+    geig = column(geig_ref[...])
+    for m in range(8):
+        block = ebuf[m // 2, 2 * (m % 2):2 * (m % 2) + 2, :, 0].astype(F32)
+        block = block[0, 0] + block[0, 1] + block[1, 0] + block[1, 1]
+        eig_row = block[0:1] + block[1:2] + block[2:3]
+        recip[:, 128 * m:128 * m + 128] = 1.0 / (geig * eig_row + 0.1)
+
+    high_parts, low_parts = [], []
+    for j in range(CHUNKS):
+        ry[j].wait_recv()
+        total = sendy[j].astype(F32)
+        for i in range(len(DY)):
+            total = total + recvy[j, i].astype(F32)
+        high_parts.append(total.astype(BF))
+        low_parts.append((total - total.astype(BF).astype(F32)).astype(BF))
+    columns = ebuf[:, :, :, 1:3].reshape(D, 128)
+    product = dot(
+        jnp.concatenate(
+            [jnp.concatenate(high_parts, axis=1), jnp.concatenate(low_parts, axis=1)], axis=0
+        ),
+        columns,
+    )
+    gbuf[c * NX + x, z] = (product[0:16] + product[16:32]).astype(BF)
+    mine = gbuf.at[c * NX + x]
+    gz = gather(mine.at[z], all_z, gbuf.at[0, pl.ds(0, 7)])
 
     psib.wait_recv()
     for i in range(2):
@@ -300,37 +354,10 @@
             ssend[k, i] = rows[:, 128 * k:128 * k + 128].astype(BF)
     sy = send([(ssend.at[(y + s) % NY], srecv.at[i], to_y(s)) for i, s in enumerate(DY)], srecv)
 
-    high_parts, low_parts = [], []
-    for j in range(CHUNKS):
-        ry[j].wait_recv()
-        total = sendy[j].astype(F32)
-        for i in range(len(DY)):
-            total = total + recvy[j, i].astype(F32)
-        high_parts.append(total.astype(BF))
-        low_parts.append((total - total.astype(BF).astype(F32)).astype(BF))
-    esib.wait_recv()
-    columns = ebuf[:, :, :, 1:3].reshape(D, 128)
-    product = dot(
-        jnp.concatenate(
-            [jnp.concatenate(high_parts, axis=1), jnp.concatenate(low_parts, axis=1)], axis=0
-        ),
-        columns,
-    )
-    gbuf[c * NX + x, z] = (product[0:16] + product[16:32]).astype(BF)
-    mine = gbuf.at[c * NX + x]
-    gz = gather(mine.at[z], all_z, gbuf.at[0, pl.ds(0, 7)])
-    b_over_z = second_z(bbuf, b_first)
-
-    geig = column(geig_ref[...])
-    for m in range(8):
-        block = ebuf[m // 2, 2 * (m % 2):2 * (m % 2) + 2, :, 0].astype(F32)
-        block = block[0, 0] + block[0, 1] + block[1, 0] + block[1, 1]
-        eig_row = block[0:1] + block[1:2] + block[2:3]
-        recip[:, 128 * m:128 * m + 128] = 1.0 / (geig * eig_row + 0.1)
-
+    b_onward = onward(bbuf, b_over_x, b_over_z)
     gz.wait_recv()
     gxc = gather(mine, all_xc, gbuf.at[pl.ds(0, 7)])
-    a_third = third(abuf, (a_over_x, a_over_z))
+    a_third = third(abuf, a_onward)
 
     sy.wait_recv()
     stat = ssend[y].astype(F32)
@@ -349,7 +376,7 @@
         total = total + dot(a_ref[:, cols], scaled, NT)
     qbuf[y] = total.astype(BF)
     qy = gather(qbuf.at[y], all_y, qbuf.at[pl.ds(0, 7)])
-    b_third = third(bbuf, (b_over_x, b_over_z))
+    b_third = third(bbuf, b_onward)
 
     sz.wait_recv()
     sout[y] = (szsend[...] + szrecv[...]).astype(BF)
@@ -388,7 +415,7 @@
 ):
     vmem = pl.BlockSpec(memory_space=pltpu.VMEM)
     hbm = pl.BlockSpec(memory_space=pl.ANY)
-    copies = 72
+    copies = 96
     result = pl.pallas_call(
         kernel,
         out_shape=jax.ShapeDtypeStruct((3, 32, D), F32),

time: 69.3 us -> 66.4 us (0.958)
  Pallas kernels: 68.5 us -> 65.2 us
    pallas_call x1, Pallas kernels: 66.7 us -> 63.4 us  [local(): pl.pallas_call(kernel, out_shape=jax.ShapeDtypeStruct((3, 32, D), F32), i...]
where the time goes in v4:
time: 66.4 us; the launch traced here: 65.9 us
  Pallas kernels  65.2 us (98%)
    pallas_call x1, Pallas kernels, local(): pl.pallas_call(kernel, out_shape=jax.ShapeDtypeStruct((3, 32, D), F32), i...  63.4 us
    pallas_call x1, Pallas kernels, local(): pl.pallas_call(functools.partial(finish, act_scale=0.25 / total_samples,...  1.86 us

profile of v4, /device:TPU:1, one launch (start us, length us, event | category | flops | bytes accessed | tf_op | source)
XLA Modules:
  0.0 65.9 jit_solution(14036787960133728420)
XLA Ops:
  0.6 63.4 %shard_map.112.result_ref = f32[3,32,1024]{2,1,0:T(8,128)} custom-call(s32[1,2]{1,0:T(1,128)} %bitcast.4, bf16[512,1024]{1,0:T(8,128)(2,1)} %acts_hbm.1, bf16[512,1024]{1,0:T(8,128)(2,1)} %grads_hbm.1, bf16[32,1024]{1,0:T(8,128)(2,1)} %a_hbm.1, bf16[32,1024]{1,0:T(8,128)(2,1)} %b_hbm.1, f32[1,32]{1,0:T(1,128)} %bitcast.5, f32[1,1024]{1,0:T(1,128)} %bitcast.3), custom_call_target="tpu_custom_call" | custom-call | flops 2147483648 | bytes 2097152 | tf_op jit(solution)/shard_map/pallas_call | solution.py:419
  64.0 1.9 %shard_map.113 = (f32[32,1024]{1,0:T(8,128)}, f32[32,1024]{1,0:T(8,128)}, f32[32,1024]{1,0:T(8,128)}) custom-call(f32[3,32,1024]{2,1,0:T(8,128)} %shard_map.112.result_ref, f32[32,1024]{1,0:T(8,128)} %old_act_ref.1, f32[32,1024]{1,0:T(8,128)} %old_grad_ref.1), custom_call_target="tpu_custom_call" | custom-call | tf_op jit(solution)/shard_map/pallas_call | solution.py:477

commit v5 on v4

--- a/solution.py
+++ b/solution.py
@@ -10,7 +10,9 @@
 NX, NY, NZ, ZL = 4, 8, 8, 4
 D, TOK = 1024, 512
 HALF = D // 2
-CHUNKS, CW = 4, 256
+WIDTHS = (384, 256, 256, 128)
+STARTS = (0, 384, 640, 896)
+CHUNKS = len(WIDTHS)
 BF, F32 = jnp.bfloat16, jnp.float32
 DX = (2, 1, 3)
 DY = (4, 3, 5, 2, 6, 1, 7)
@@ -139,8 +141,8 @@
     acts_sib = send([(half(acts_hbm, 1 - c), acts_sv, sibling)], acts_sv)
     grads_sib = []
     for j in range(CHUNKS):
-        piece = grads_v.at[1, :, pl.ds(CW * j, CW)]
-        grads_sib.append(send([(grads_hbm.at[:, pl.ds(CW * j, CW)], piece, sibling)], piece))
+        piece = grads_v.at[1, :, pl.ds(STARTS[j], WIDTHS[j])]
+        grads_sib.append(send([(grads_hbm.at[:, pl.ds(STARTS[j], WIDTHS[j])], piece, sibling)], piece))
     for copy in own:
         copy.start()
 
@@ -206,12 +208,12 @@
 
     def term(slot, j):
         part = dot(
-            actst[:, slot * TOK:slot * TOK + TOK], grads_v[slot, :, CW * j:CW * j + CW]
+            actst[:, slot * TOK:slot * TOK + TOK], grads_v[slot, :, STARTS[j]:STARTS[j] + WIDTHS[j]]
         )
-        return part.reshape(NX, 128, CW)
+        return part.reshape(NX, 128, WIDTHS[j])
 
     for j in range(CHUNKS):
-        tbuf[j] = term(0, j)
+        tbuf[j][...] = term(0, j)
     acts_sib.wait_recv()
     for k in range(2):
         for t in range(2):
@@ -236,22 +238,22 @@
 
     def forward(j):
         r1[j][0].wait_recv()
-        sendx2[j, 0] = (tbuf[j, x_up, 0:64, :] + recvx1[j, 0, 0].astype(F32)).astype(BF)
-        up = send([(sendx2.at[j, 0], recvx2.at[j, 0], to_x(1))], recvx2.at[j, 0])
+        sendx2[j][0] = (tbuf[j][x_up, 0:64, :] + recvx1[j][0, 0].astype(F32)).astype(BF)
+        up = send([(sendx2[j].at[0], recvx2[j].at[0], to_x(1))], recvx2[j].at[0])
         r1[j][1].wait_recv()
-        sendx2[j, 1] = (tbuf[j, x_down, 64:128, :] + recvx1[j, 1, 0].astype(F32)).astype(BF)
-        down = send([(sendx2.at[j, 1], recvx2.at[j, 1], to_x(3))], recvx2.at[j, 1])
+        sendx2[j][1] = (tbuf[j][x_down, 64:128, :] + recvx1[j][1, 0].astype(F32)).astype(BF)
+        down = send([(sendx2[j].at[1], recvx2[j].at[1], to_x(3))], recvx2[j].at[1])
         r2[j] = (up, down)
 
     for j in range(CHUNKS):
         grads_sib[j].wait_recv()
-        tbuf[j] = tbuf[j] + term(1, j)
-        sendx1[j, 0, 0] = tbuf[j, x_far, 0:64, :].astype(BF)
-        sendx1[j, 0, 1] = tbuf[j, x_up, 64:128, :].astype(BF)
-        sendx1[j, 1, 0] = tbuf[j, x_far, 64:128, :].astype(BF)
-        sendx1[j, 1, 1] = tbuf[j, x_down, 0:64, :].astype(BF)
+        tbuf[j][...] = tbuf[j][...] + term(1, j)
+        sendx1[j][0, 0] = tbuf[j][x_far, 0:64, :].astype(BF)
+        sendx1[j][0, 1] = tbuf[j][x_up, 64:128, :].astype(BF)
+        sendx1[j][1, 0] = tbuf[j][x_far, 64:128, :].astype(BF)
+        sendx1[j][1, 1] = tbuf[j][x_down, 0:64, :].astype(BF)
         r1[j] = [
-            send([(sendx1.at[j, i], recvx1.at[j, i], to_x(s))], recvx1.at[j, i])
+            send([(sendx1[j].at[i], recvx1[j].at[i], to_x(s))], recvx1[j].at[i])
             for i, s in enumerate((1, 3))
         ]
         if j == 2:
@@ -276,23 +278,23 @@
     def sum_x(j):
         r2[j][0].wait_recv()
         r2[j][1].wait_recv()
-        top = tbuf[j, x, 0:64, :] + recvx1[j, 1, 1].astype(F32) + recvx2[j, 0].astype(F32)
-        low = tbuf[j, x, 64:128, :] + recvx1[j, 0, 1].astype(F32) + recvx2[j, 1].astype(F32)
-        sendz[j, 0:4] = top.astype(BF).reshape(4, 16, CW)
-        sendz[j, 4:8] = low.astype(BF).reshape(4, 16, CW)
+        top = tbuf[j][x, 0:64, :] + recvx1[j][1, 1].astype(F32) + recvx2[j][0].astype(F32)
+        low = tbuf[j][x, 64:128, :] + recvx1[j][0, 1].astype(F32) + recvx2[j][1].astype(F32)
+        sendz[j][0:4] = top.astype(BF).reshape(4, 16, WIDTHS[j])
+        sendz[j][4:8] = low.astype(BF).reshape(4, 16, WIDTHS[j])
         rz[j] = send(
-            [(sendz.at[j, (z + s) % NZ], recvz.at[j, i], to_z(s)) for i, s in enumerate(DZ)],
-            recvz.at[j],
+            [(sendz[j].at[(z + s) % NZ], recvz[j].at[i], to_z(s)) for i, s in enumerate(DZ)],
+            recvz[j],
         )
 
     def sum_z(j):
         rz[j].wait_recv()
-        total = sendz[j, z].astype(F32)
+        total = sendz[j][z].astype(F32)
         for i in range(len(DZ)):
-            total = total + recvz[j, i].astype(F32)
-        sendy[j] = total.astype(BF)
+            total = total + recvz[j][i].astype(F32)
+        sendy[j][...] = total.astype(BF)
         ry[j] = send(
-            [(sendy.at[j], recvy.at[j, i], to_y(s)) for i, s in enumerate(DY)], recvy.at[j]
+            [(sendy[j], recvy[j].at[i], to_y(s)) for i, s in enumerate(DY)], recvy[j]
         )
 
     sum_x(0)
@@ -323,9 +325,9 @@
     high_parts, low_parts = [], []
     for j in range(CHUNKS):
         ry[j].wait_recv()
-        total = sendy[j].astype(F32)
+        total = sendy[j][...].astype(F32)
         for i in range(len(DY)):
-            total = total + recvy[j, i].astype(F32)
+            total = total + recvy[j][i].astype(F32)
         high_parts.append(total.astype(BF))
         low_parts.append((total - total.astype(BF).astype(F32)).astype(BF))
     columns = ebuf[:, :, :, 1:3].reshape(D, 128)
@@ -338,6 +340,7 @@
     gbuf[c * NX + x, z] = (product[0:16] + product[16:32]).astype(BF)
     mine = gbuf.at[c * NX + x]
     gz = gather(mine.at[z], all_z, gbuf.at[0, pl.ds(0, 7)])
+    a_third = third(abuf, a_onward)
 
     psib.wait_recv()
     for i in range(2):
@@ -357,7 +360,7 @@
     b_onward = onward(bbuf, b_over_x, b_over_z)
     gz.wait_recv()
     gxc = gather(mine, all_xc, gbuf.at[pl.ds(0, 7)])
-    a_third = third(abuf, a_onward)
+    b_third = third(bbuf, b_onward)
 
     sy.wait_recv()
     stat = ssend[y].astype(F32)
@@ -376,7 +379,6 @@
         total = total + dot(a_ref[:, cols], scaled, NT)
     qbuf[y] = total.astype(BF)
     qy = gather(qbuf.at[y], all_y, qbuf.at[pl.ds(0, 7)])
-    b_third = third(bbuf, b_onward)
 
     sz.wait_recv()
     sout[y] = (szsend[...] + szrecv[...]).astype(BF)
@@ -432,15 +434,15 @@
             pltpu.VMEM((HALF, 2 * TOK), BF),
             pltpu.VMEM((4, NX, ZL, 64, 256), BF),
             pltpu.VMEM((4, NX, ZL, 64, 256), BF),
-            pltpu.VMEM((CHUNKS, NX, 128, CW), F32),
-            pltpu.VMEM((CHUNKS, 2, 2, 64, CW), BF),
-            pltpu.VMEM((CHUNKS, 2, 2, 64, CW), BF),
-            pltpu.VMEM((CHUNKS, 2, 64, CW), BF),
-            pltpu.VMEM((CHUNKS, 2, 64, CW), BF),
-            pltpu.VMEM((CHUNKS, NZ, 16, CW), BF),
-            pltpu.VMEM((CHUNKS, 7, 16, CW), BF),
-            pltpu.VMEM((CHUNKS, 16, CW), BF),
-            pltpu.VMEM((CHUNKS, 7, 16, CW), BF),
+            [pltpu.VMEM((NX, 128, w), F32) for w in WIDTHS],
+            [pltpu.VMEM((2, 2, 64, w), BF) for w in WIDTHS],
+            [pltpu.VMEM((2, 2, 64, w), BF) for w in WIDTHS],
+            [pltpu.VMEM((2, 64, w), BF) for w in WIDTHS],
+            [pltpu.VMEM((2, 64, w), BF) for w in WIDTHS],
+            [pltpu.VMEM((NZ, 16, w), BF) for w in WIDTHS],
+            [pltpu.VMEM((7, 16, w), BF) for w in WIDTHS],
+            [pltpu.VMEM((16, w), BF) for w in WIDTHS],
+            [pltpu.VMEM((7, 16, w), BF) for w in WIDTHS],
             pltpu.VMEM((2 * NX, NZ, 16, 128), BF),
             pltpu.VMEM((128, D), F32),
             pltpu.VMEM((NY, 32, 128), BF),

time: 66.4 us -> 67.2 us (1.012)
  no operation moved by 1% of the time
where the time goes in v5:
time: 67.2 us; the launch traced here: 66 us
  Pallas kernels  65.4 us (97%)
    pallas_call x1, Pallas kernels, local(): pl.pallas_call(kernel, out_shape=jax.ShapeDtypeStruct((3, 32, D), F32), i...  63.5 us
    pallas_call x1, Pallas kernels, local(): pl.pallas_call(functools.partial(finish, act_scale=0.25 / total_samples,...  1.86 us

profile of v5, /device:TPU:1, one launch (start us, length us, event | category | flops | bytes accessed | tf_op | source)
XLA Modules:
  0.0 66.0 jit_solution(14069567488069323455)
XLA Ops:
  0.6 63.5 %shard_map.112.result_ref = f32[3,32,1024]{2,1,0:T(8,128)} custom-call(s32[1,2]{1,0:T(1,128)} %bitcast.4, bf16[512,1024]{1,0:T(8,128)(2,1)} %acts_hbm.1, bf16[512,1024]{1,0:T(8,128)(2,1)} %grads_hbm.1, bf16[32,1024]{1,0:T(8,128)(2,1)} %a_hbm.1, bf16[32,1024]{1,0:T(8,128)(2,1)} %b_hbm.1, f32[1,32]{1,0:T(1,128)} %bitcast.5, f32[1,1024]{1,0:T(1,128)} %bitcast.3), custom_call_target="tpu_custom_call" | custom-call | flops 2147483648 | bytes 2097152 | tf_op jit(solution)/shard_map/pallas_call | solution.py:421
  64.2 1.9 %shard_map.113 = (f32[32,1024]{1,0:T(8,128)}, f32[32,1024]{1,0:T(8,128)}, f32[32,1024]{1,0:T(8,128)}) custom-call(f32[3,32,1024]{2,1,0:T(8,128)} %shard_map.112.result_ref, f32[32,1024]{1,0:T(8,128)} %old_act_ref.1, f32[32,1024]{1,0:T(8,128)} %old_grad_ref.1), custom_call_target="tpu_custom_call" | custom-call | tf_op jit(solution)/shard_map/pallas_call | solution.py:479

commit v6 on v4

--- a/solution.py
+++ b/solution.py
@@ -34,9 +34,9 @@
     idx_hbm, acts_hbm, grads_hbm, a_hbm, b_hbm, aeig_hbm, geig_hbm,
     out_ref,
     idx_ref, a_ref, aeig_ref, geig_ref,
-    acts_v, acts_sv, grads_v, actst, abuf, bbuf,
+    acts_v, acts_sv, grads_v, actst, abuf,
     tbuf, sendx1, recvx1, sendx2, recvx2, sendz, recvz, sendy, recvy,
-    gbuf, recip, qbuf,
+    gbuf, recip, qsend, qrecv, qbuf,
     shifted, parts, ebuf, picks, pbuf, pwide, xbuf, sfull, ssend, srecv, szsend, szrecv, sout,
     lsem, ssem, rsem,
 ):
@@ -120,22 +120,18 @@
         (acts_hbm, acts_v), (grads_hbm, grads_v.at[0]), (idx_hbm, idx_ref),
         (geig_hbm.at[:, my_cols], geig_ref), (a_hbm, a_ref),
     ]
-    for source, whole in ((a_hbm, abuf), (b_hbm, bbuf)):
-        for h in range(2):
-            moves.append((quarter(source, c, h), whole.at[2 * c + h, x, zl, my_rows]))
+    for h in range(2):
+        moves.append((quarter(a_hbm, c, h), abuf.at[2 * c + h, x, zl, my_rows]))
     own = [pltpu.make_async_copy(src, dst, lsem.at[i]) for i, (src, dst) in enumerate(moves)]
     pl.semaphore_wait(barrier, len(partners))
 
-    basis_sib = []
-    for source, whole in ((a_hbm, abuf), (b_hbm, bbuf)):
-        basis_sib.append(send(
-            [
-                (quarter(source, 1 - c, h), whole.at[2 * (1 - c) + h, x, zl, my_rows], sibling)
-                for h in range(2)
-            ],
-            whole.at[pl.ds(0, 2), 0, 0, pl.ds(0, 32)],
-        ))
-
+    basis_sib = send(
+        [
+            (quarter(a_hbm, 1 - c, h), abuf.at[2 * (1 - c) + h, x, zl, my_rows], sibling)
+            for h in range(2)
+        ],
+        abuf.at[pl.ds(0, 2), 0, 0, pl.ds(0, 32)],
+    )
     acts_sib = send([(half(acts_hbm, 1 - c), acts_sv, sibling)], acts_sv)
     grads_sib = []
     for j in range(CHUNKS):
@@ -201,7 +197,7 @@
 
     for copy in own[4:]:
         copy.wait()
-    basis_sib[0].wait_recv()
+    basis_sib.wait_recv()
     a_first = first(abuf)
 
     def term(slot, j):
@@ -268,8 +264,6 @@
     px = gather(pbuf.at[x, :, c], all_x, pbuf.at[pl.ds(0, 3), :, 0])
     a_first[0].wait_recv()
     a_over_x = near_x(abuf)
-    basis_sib[1].wait_recv()
-    b_first = first(bbuf)
 
     rz, ry = {}, {}
 
@@ -305,10 +299,7 @@
     ex.wait_recv()
     esib = gather(ebuf.at[:, :, c], [sibling], ebuf.at[:, :, c])
     sum_z(3)
-    for copy in b_first:
-        copy.wait_recv()
     a_onward = onward(abuf, a_over_x, a_over_z)
-    b_over_x, b_over_z = near_x(bbuf), near_z(bbuf)
     px.wait_recv()
     psib = gather(pbuf.at[:, :, c], [sibling], pbuf.at[:, :, c])
 
@@ -354,7 +345,6 @@
             ssend[k, i] = rows[:, 128 * k:128 * k + 128].astype(BF)
     sy = send([(ssend.at[(y + s) % NY], srecv.at[i], to_y(s)) for i, s in enumerate(DY)], srecv)
 
-    b_onward = onward(bbuf, b_over_x, b_over_z)
     gz.wait_recv()
     gxc = gather(mine, all_xc, gbuf.at[pl.ds(0, 7)])
     a_third = third(abuf, a_onward)
@@ -374,32 +364,37 @@
         cols = slice(256 * q, 256 * q + 256)
         scaled = (dot(turned, abuf[q].reshape(D, 256)) * recip[:, cols]).astype(BF)
         total = total + dot(a_ref[:, cols], scaled, NT)
-    qbuf[y] = total.astype(BF)
-    qy = gather(qbuf.at[y], all_y, qbuf.at[pl.ds(0, 7)])
-    b_third = third(bbuf, b_onward)
+    high = total.astype(BF)
+    low = (total - high.astype(F32)).astype(BF)
+    partial = dot(jnp.concatenate([high, low], axis=0), columns, NT)
+    partial = partial[0:32] + partial[32:64]
+    for k in range(8):
+        qsend[k] = partial[:, 128 * k:128 * k + 128].astype(BF)
+    qr = send([(qsend.at[(y + s) % NY], qrecv.at[i], to_y(s)) for i, s in enumerate(DY)], qrecv)
 
     sz.wait_recv()
     sout[y] = (szsend[...] + szrecv[...]).astype(BF)
     so = gather(sout.at[y], all_y, sout.at[pl.ds(0, 7)])
+    qr.wait_recv()
+    total = qsend[y].astype(F32)
+    for i in range(len(DY)):
+        total = total + qrecv[i].astype(F32)
+    qbuf[y] = total.astype(BF)
+    qy = gather(qbuf.at[y], all_y, qbuf.at[pl.ds(0, 7)])
     drain()
-
-    qy.wait_recv()
-    left = jnp.concatenate([qbuf[k] for k in range(8)], axis=1)
-    b_third.wait_recv()
-    total = dot(left[:, 0:256], bbuf[0].reshape(D, 256), NT)
-    for q in range(1, 4):
-        total = total + dot(left[:, 256 * q:256 * q + 256], bbuf[q].reshape(D, 256), NT)
-    out_ref[0] = total
     so.wait_recv()
     for i in range(2):
         for k in range(8):
-            out_ref[1 + i, :, 128 * k:128 * k + 128] = sout[k, i].astype(F32)
+            out_ref[1 + i, :, 128 * k:128 * k + 128] = sout[k, i]
+    qy.wait_recv()
+    for k in range(8):
+        out_ref[0, :, 128 * k:128 * k + 128] = qbuf[k]
 
 
 def finish(result_ref, old_act_ref, old_grad_ref, pre_ref, act_ref, grad_ref, *, act_scale, grad_scale):
-    pre_ref[...] = result_ref[0]
-    act_ref[...] = 0.75 * old_act_ref[...] + act_scale * result_ref[1]
-    grad_ref[...] = 0.75 * old_grad_ref[...] + grad_scale * result_ref[2]
+    pre_ref[...] = result_ref[0].astype(F32)
+    act_ref[...] = 0.75 * old_act_ref[...] + act_scale * result_ref[1].astype(F32)
+    grad_ref[...] = 0.75 * old_grad_ref[...] + grad_scale * result_ref[2].astype(F32)
 
 
 def local(
@@ -418,7 +413,7 @@
     copies = 96
     result = pl.pallas_call(
         kernel,
-        out_shape=jax.ShapeDtypeStruct((3, 32, D), F32),
+        out_shape=jax.ShapeDtypeStruct((3, 32, D), BF),
         in_specs=[hbm] * 7,
         out_specs=vmem,
         scratch_shapes=[
@@ -431,7 +426,6 @@
             pltpu.VMEM((2, TOK, D), BF),
             pltpu.VMEM((HALF, 2 * TOK), BF),
             pltpu.VMEM((4, NX, ZL, 64, 256), BF),
-            pltpu.VMEM((4, NX, ZL, 64, 256), BF),
             pltpu.VMEM((CHUNKS, NX, 128, CW), F32),
             pltpu.VMEM((CHUNKS, 2, 2, 64, CW), BF),
             pltpu.VMEM((CHUNKS, 2, 2, 64, CW), BF),
@@ -443,6 +437,8 @@
             pltpu.VMEM((CHUNKS, 7, 16, CW), BF),
             pltpu.VMEM((2 * NX, NZ, 16, 128), BF),
             pltpu.VMEM((128, D), F32),
+            pltpu.VMEM((NY, 32, 128), BF),
+            pltpu.VMEM((7, 32, 128), BF),
             pltpu.VMEM((NY, 32, 128), BF),
             pltpu.VMEM((8, 128), F32),
             pltpu.VMEM((16, 128), F32),

time: 66.4 us -> 66.5 us (level)
  no operation moved by 1% of the time
where the time goes in v6:
time: 66.5 us; the launch traced here: 66.3 us
  Pallas kernels  65.7 us (99%)
    pallas_call x1, Pallas kernels, local(): pl.pallas_call(kernel, out_shape=jax.ShapeDtypeStruct((3, 32, D), BF), in...  63.9 us
    pallas_call x1, Pallas kernels, local(): pl.pallas_call(functools.partial(finish, act_scale=0.25 / total_samples,...  1.83 us

profile of v6, /device:TPU:1, one launch (start us, length us, event | category | flops | bytes accessed | tf_op | source)
XLA Modules:
  0.0 66.3 jit_solution(9689475512087496838)
XLA Ops:
  0.6 63.9 %shard_map.112.result_ref = bf16[3,32,1024]{2,1,0:T(8,128)(2,1)} custom-call(s32[1,2]{1,0:T(1,128)} %bitcast.4, bf16[512,1024]{1,0:T(8,128)(2,1)} %acts_hbm.1, bf16[512,1024]{1,0:T(8,128)(2,1)} %grads_hbm.1, bf16[32,1024]{1,0:T(8,128)(2,1)} %a_hbm.1, bf16[32,1024]{1,0:T(8,128)(2,1)} %b_hbm.1, f32[1,32]{1,0:T(1,128)} %bitcast.5, f32[1,1024]{1,0:T(1,128)} %bitcast.3), custom_call_target="tpu_custom_call" | custom-call | flops 2147483648 | bytes 2097152 | tf_op jit(solution)/shard_map/pallas_call | solution.py:414
  64.5 1.8 %shard_map.113 = (f32[32,1024]{1,0:T(8,128)}, f32[32,1024]{1,0:T(8,128)}, f32[32,1024]{1,0:T(8,128)}) custom-call(bf16[3,32,1024]{2,1,0:T(8,128)(2,1)} %shard_map.112.result_ref, f32[32,1024]{1,0:T(8,128)} %old_act_ref.1, f32[32,1024]{1,0:T(8,128)} %old_grad_ref.1), custom_call_target="tpu_custom_call" | custom-call | tf_op jit(solution)/shard_map/pallas_call | solution.py:473

commit v7 on v6

--- a/solution.py
+++ b/solution.py
@@ -97,13 +97,6 @@
     x_up, x_down, x_far = (x + 1) % NX, (x + 3) % NX, (x + 2) % NX
     zl_up, zl_down = (zl + 1) % ZL, (zl + 3) % ZL
 
-    barrier = pltpu.get_barrier_semaphore()
-    partners = all_xc + all_y + all_z
-    for partner in partners:
-        pl.semaphore_signal(
-            barrier, inc=1, device_id=partner, device_id_type=pl.DeviceIdType.MESH
-        )
-
     my_rows = pl.ds(pl.multiple_of(c * 32, 32), 32)
     my_cols = pl.ds(pl.multiple_of(y * 128, 128), 128)
 
@@ -123,6 +116,16 @@
     for h in range(2):
         moves.append((quarter(a_hbm, c, h), abuf.at[2 * c + h, x, zl, my_rows]))
     own = [pltpu.make_async_copy(src, dst, lsem.at[i]) for i, (src, dst) in enumerate(moves)]
+    for copy in own[3:5]:
+        copy.start()
+
+    barrier = pltpu.get_barrier_semaphore()
+    partners = all_xc + all_y + all_z
+    for partner in partners:
+        pl.semaphore_signal(
+            barrier, inc=1, device_id=partner, device_id_type=pl.DeviceIdType.MESH
+        )
+
     pl.semaphore_wait(barrier, len(partners))
 
     basis_sib = send(
@@ -137,8 +140,16 @@
     for j in range(CHUNKS):
         piece = grads_v.at[1, :, pl.ds(CW * j, CW)]
         grads_sib.append(send([(grads_hbm.at[:, pl.ds(CW * j, CW)], piece, sibling)], piece))
-    for copy in own:
+    for copy in own[:3] + own[5:]:
         copy.start()
+
+    own[3].wait()
+    mine = acts_v[:, pl.ds(pl.multiple_of(c * HALF, HALF), HALF)]
+    for k in range(2):
+        for t in range(2):
+            actst[256 * k:256 * k + 256, 256 * t:256 * t + 256] = (
+                mine[256 * t:256 * t + 256, 256 * k:256 * k + 256].T
+            )
 
     own[0].wait()
     shifted[...] = jnp.zeros((8, 128), F32)
@@ -154,14 +165,6 @@
     for copy in own[1:3]:
         copy.wait()
     ez = gather(ebuf.at[x, zl, c], all_zl, ebuf.at[0, pl.ds(0, 3), 0])
-
-    own[3].wait()
-    mine = acts_v[:, pl.ds(pl.multiple_of(c * HALF, HALF), HALF)]
-    for k in range(2):
-        for t in range(2):
-            actst[256 * k:256 * k + 256, 256 * t:256 * t + 256] = (
-                mine[256 * t:256 * t + 256, 256 * k:256 * k + 256].T
-            )
 
     def first(whole):
         return (
@@ -298,11 +301,10 @@
     sum_z(2)
     ex.wait_recv()
     esib = gather(ebuf.at[:, :, c], [sibling], ebuf.at[:, :, c])
+    px.wait_recv()
+    psib = gather(pbuf.at[:, :, c], [sibling], pbuf.at[:, :, c])
     sum_z(3)
     a_onward = onward(abuf, a_over_x, a_over_z)
-    px.wait_recv()
-    psib = gather(pbuf.at[:, :, c], [sibling], pbuf.at[:, :, c])
-
     esib.wait_recv()
     geig = column(geig_ref[...])
     for m in range(8):
@@ -310,6 +312,21 @@
         block = block[0, 0] + block[0, 1] + block[1, 0] + block[1, 1]
         eig_row = block[0:1] + block[1:2] + block[2:3]
         recip[:, 128 * m:128 * m + 128] = 1.0 / (geig * eig_row + 0.1)
+
+    psib.wait_recv()
+    for i in range(2):
+        pwide[...] = pbuf[:, :, :, i].reshape(2 * NX * ZL * 16, 128).astype(F32)
+        for k in range(8):
+            part = jnp.concatenate(
+                [pwide[pl.ds(s * 8 + k, 2 * NX * ZL, stride=16), :] for s in range(2)], axis=0
+            )
+            xbuf[k] = part.astype(BF)
+        wide = jnp.concatenate([xbuf[k] for k in range(8)], axis=1)
+        sfull[...] = dot(xbuf[dev // 4], wide, (((0,), (0,)), ((), ())))
+        rows = sfull[pl.ds(pl.multiple_of((dev % 4) * 32, 32), 32), :]
+        for k in range(8):
+            ssend[k, i] = rows[:, 128 * k:128 * k + 128].astype(BF)
+    sy = send([(ssend.at[(y + s) % NY], srecv.at[i], to_y(s)) for i, s in enumerate(DY)], srecv)
 
     high_parts, low_parts = [], []
     for j in range(CHUNKS):
@@ -330,23 +347,6 @@
     mine = gbuf.at[c * NX + x]
     gz = gather(mine.at[z], all_z, gbuf.at[0, pl.ds(0, 7)])
 
-    psib.wait_recv()
-    for i in range(2):
-        pwide[...] = pbuf[:, :, :, i].reshape(2 * NX * ZL * 16, 128).astype(F32)
-        for k in range(8):
-            part = jnp.concatenate(
-                [pwide[pl.ds(s * 8 + k, 2 * NX * ZL, stride=16), :] for s in range(2)], axis=0
-            )
-            xbuf[k] = part.astype(BF)
-        wide = jnp.concatenate([xbuf[k] for k in range(8)], axis=1)
-        sfull[...] = dot(xbuf[dev // 4], wide, (((0,), (0,)), ((), ())))
-        rows = sfull[pl.ds(pl.multiple_of((dev % 4) * 32, 32), 32), :]
-        for k in range(8):
-            ssend[k, i] = rows[:, 128 * k:128 * k + 128].astype(BF)
-    sy = send([(ssend.at[(y + s) % NY], srecv.at[i], to_y(s)) for i, s in enumerate(DY)], srecv)
-
-    gz.wait_recv()
-    gxc = gather(mine, all_xc, gbuf.at[pl.ds(0, 7)])
     a_third = third(abuf, a_onward)
 
     sy.wait_recv()
@@ -355,6 +355,13 @@
         stat = stat + srecv[i].astype(F32)
     szsend[...] = stat
     sz = send([(szsend, szrecv, to_z(4))], szrecv)
+
+    gz.wait_recv()
+    gxc = gather(mine, all_xc, gbuf.at[pl.ds(0, 7)])
+
+    sz.wait_recv()
+    sout[y] = (szsend[...] + szrecv[...]).astype(BF)
+    so = gather(sout.at[y], all_y, sout.at[pl.ds(0, 7)])
 
     gxc.wait_recv()
     turned = gbuf[...].reshape(D, 128).T
@@ -372,9 +379,6 @@
         qsend[k] = partial[:, 128 * k:128 * k + 128].astype(BF)
     qr = send([(qsend.at[(y + s) % NY], qrecv.at[i], to_y(s)) for i, s in enumerate(DY)], qrecv)
 
-    sz.wait_recv()
-    sout[y] = (szsend[...] + szrecv[...]).astype(BF)
-    so = gather(sout.at[y], all_y, sout.at[pl.ds(0, 7)])
     qr.wait_recv()
     total = qsend[y].astype(F32)
     for i in range(len(DY)):

time: 66.5 us -> 66.6 us (level)
  the two profiles are of different devices: /device:TPU:1 before, /device:TPU:2 now
where the time goes in v7:
time: 66.6 us; the launch traced here: 66.5 us
  Pallas kernels  65.8 us (99%)
    pallas_call x1, Pallas kernels, local(): pl.pallas_call(kernel, out_shape=jax.ShapeDtypeStruct((3, 32, D), BF), in...  64 us
    pallas_call x1, Pallas kernels, local(): pl.pallas_call(functools.partial(finish, act_scale=0.25 / total_samples,...  1.83 us

profile of v7, /device:TPU:2, one launch (start us, length us, event | category | flops | bytes accessed | tf_op | source)
XLA Modules:
  0.0 66.5 jit_solution(16549125082062493206)
XLA Ops:
  0.6 64.0 %shard_map.112.result_ref = bf16[3,32,1024]{2,1,0:T(8,128)(2,1)} custom-call(s32[1,2]{1,0:T(1,128)} %bitcast.4, bf16[512,1024]{1,0:T(8,128)(2,1)} %acts_hbm.1, bf16[512,1024]{1,0:T(8,128)(2,1)} %grads_hbm.1, bf16[32,1024]{1,0:T(8,128)(2,1)} %a_hbm.1, bf16[32,1024]{1,0:T(8,128)(2,1)} %b_hbm.1, f32[1,32]{1,0:T(1,128)} %bitcast.5, f32[1,1024]{1,0:T(1,128)} %bitcast.3), custom_call_target="tpu_custom_call" | custom-call | flops 2147483648 | bytes 2097152 | tf_op jit(solution)/shard_map/pallas_call | solution.py:418
  64.6 1.8 %shard_map.113 = (f32[32,1024]{1,0:T(8,128)}, f32[32,1024]{1,0:T(8,128)}, f32[32,1024]{1,0:T(8,128)}) custom-call(bf16[3,32,1024]{2,1,0:T(8,128)(2,1)} %shard_map.112.result_ref, f32[32,1024]{1,0:T(8,128)} %old_act_ref.1, f32[32,1024]{1,0:T(8,128)} %old_grad_ref.1), custom_call_target="tpu_custom_call" | custom-call | tf_op jit(solution)/shard_map/pallas_call | solution.py:477

commit v8 on v7

--- a/solution.py
+++ b/solution.py
@@ -10,7 +10,7 @@
 NX, NY, NZ, ZL = 4, 8, 8, 4
 D, TOK = 1024, 512
 HALF = D // 2
-CHUNKS, CW = 4, 256
+CHUNKS, CW = 2, 512
 BF, F32 = jnp.bfloat16, jnp.float32
 DX = (2, 1, 3)
 DY = (4, 3, 5, 2, 6, 1, 7)
@@ -253,14 +253,11 @@
             send([(sendx1.at[j, i], recvx1.at[j, i], to_x(s))], recvx1.at[j, i])
             for i, s in enumerate((1, 3))
         ]
-        if j == 2:
-            a_first[1].wait_recv()
-            a_over_z = near_z(abuf)
-            pz = pick()
-        if j > 1:
-            forward(j - 2)
-    forward(CHUNKS - 2)
-    forward(CHUNKS - 1)
+    a_first[1].wait_recv()
+    a_over_z = near_z(abuf)
+    pz = pick()
+    for j in range(CHUNKS):
+        forward(j)
     ez.wait_recv()
     ex = gather(ebuf.at[x, :, c], all_x, ebuf.at[pl.ds(0, 3), :, 0])
     pz.wait_recv()
@@ -295,15 +292,11 @@
     sum_x(0)
     sum_x(1)
     sum_z(0)
-    sum_x(2)
-    sum_z(1)
-    sum_x(3)
-    sum_z(2)
     ex.wait_recv()
     esib = gather(ebuf.at[:, :, c], [sibling], ebuf.at[:, :, c])
     px.wait_recv()
     psib = gather(pbuf.at[:, :, c], [sibling], pbuf.at[:, :, c])
-    sum_z(3)
+    sum_z(1)
     a_onward = onward(abuf, a_over_x, a_over_z)
     esib.wait_recv()
     geig = column(geig_ref[...])

time: 66.6 us -> 66.7 us (level)
  the two profiles are of different devices: /device:TPU:2 before, /device:TPU:1 now
where the time goes in v8:
time: 66.7 us; the launch traced here: 65.7 us
  Pallas kernels  65 us (97%)
    pallas_call x1, Pallas kernels, local(): pl.pallas_call(kernel, out_shape=jax.ShapeDtypeStruct((3, 32, D), BF), in...  63.2 us
    pallas_call x1, Pallas kernels, local(): pl.pallas_call(functools.partial(finish, act_scale=0.25 / total_samples,...  1.83 us

profile of v8, /device:TPU:1, one launch (start us, length us, event | category | flops | bytes accessed | tf_op | source)
XLA Modules:
  0.0 65.7 jit_solution(18012165320154757814)
XLA Ops:
  0.6 63.2 %shard_map.112.result_ref = bf16[3,32,1024]{2,1,0:T(8,128)(2,1)} custom-call(s32[1,2]{1,0:T(1,128)} %bitcast.4, bf16[512,1024]{1,0:T(8,128)(2,1)} %acts_hbm.1, bf16[512,1024]{1,0:T(8,128)(2,1)} %grads_hbm.1, bf16[32,1024]{1,0:T(8,128)(2,1)} %a_hbm.1, bf16[32,1024]{1,0:T(8,128)(2,1)} %b_hbm.1, f32[1,32]{1,0:T(1,128)} %bitcast.5, f32[1,1024]{1,0:T(1,128)} %bitcast.3), custom_call_target="tpu_custom_call" | custom-call | flops 2147483648 | bytes 2097152 | tf_op jit(solution)/shard_map/pallas_call | solution.py:411
  63.8 1.8 %shard_map.113 = (f32[32,1024]{1,0:T(8,128)}, f32[32,1024]{1,0:T(8,128)}, f32[32,1024]{1,0:T(8,128)}) custom-call(bf16[3,32,1024]{2,1,0:T(8,128)(2,1)} %shard_map.112.result_ref, f32[32,1024]{1,0:T(8,128)} %old_act_ref.1, f32[32,1024]{1,0:T(8,128)} %old_grad_ref.1), custom_call_target="tpu_custom_call" | custom-call | tf_op jit(solution)/shard_map/pallas_call | solution.py:470

commit v9 on v7

--- a/solution.py
+++ b/solution.py
@@ -34,7 +34,7 @@
     idx_hbm, acts_hbm, grads_hbm, a_hbm, b_hbm, aeig_hbm, geig_hbm,
     out_ref,
     idx_ref, a_ref, aeig_ref, geig_ref,
-    acts_v, acts_sv, grads_v, actst, abuf,
+    acts_v, grads_v, actst, sendc, recvc, abuf,
     tbuf, sendx1, recvx1, sendx2, recvx2, sendz, recvz, sendy, recvy,
     gbuf, recip, qsend, qrecv, qbuf,
     shifted, parts, ebuf, picks, pbuf, pwide, xbuf, sfull, ssend, srecv, szsend, szrecv, sout,
@@ -100,9 +100,6 @@
     my_rows = pl.ds(pl.multiple_of(c * 32, 32), 32)
     my_cols = pl.ds(pl.multiple_of(y * 128, 128), 128)
 
-    def half(ref, side):
-        return ref.at[:, pl.ds(pl.multiple_of(side * HALF, HALF), HALF)]
-
     def quarter(ref, side, h):
         return ref.at[:, pl.ds(pl.multiple_of(side * HALF + h * 256, 256), 256)]
 
@@ -110,7 +107,7 @@
         (aeig_hbm, aeig_ref),
         (b_hbm.at[pl.ds(0, 16), my_cols], ebuf.at[x, zl, c, 1]),
         (b_hbm.at[pl.ds(16, 16), my_cols], ebuf.at[x, zl, c, 2]),
-        (acts_hbm, acts_v), (grads_hbm, grads_v.at[0]), (idx_hbm, idx_ref),
+        (acts_hbm, acts_v), (grads_hbm, grads_v), (idx_hbm, idx_ref),
         (geig_hbm.at[:, my_cols], geig_ref), (a_hbm, a_ref),
     ]
     for h in range(2):
@@ -126,6 +123,24 @@
             barrier, inc=1, device_id=partner, device_id_type=pl.DeviceIdType.MESH
         )
 
+    for copy in own[:3] + own[5:]:
+        copy.start()
+
+    def turn(side):
+        mine = acts_v[:, pl.ds(pl.multiple_of(side * HALF, HALF), HALF)]
+        for k in range(2):
+            for t in range(2):
+                actst[256 * k:256 * k + 256, 256 * t:256 * t + 256] = (
+                    mine[256 * t:256 * t + 256, 256 * k:256 * k + 256].T
+                )
+
+    def term(j):
+        return dot(actst[...], grads_v[:, CW * j:CW * j + CW])
+
+    own[3].wait()
+    turn(1 - c)
+    own[4].wait()
+
     pl.semaphore_wait(barrier, len(partners))
 
     basis_sib = send(
@@ -135,21 +150,11 @@
         ],
         abuf.at[pl.ds(0, 2), 0, 0, pl.ds(0, 32)],
     )
-    acts_sib = send([(half(acts_hbm, 1 - c), acts_sv, sibling)], acts_sv)
-    grads_sib = []
+    rc = []
     for j in range(CHUNKS):
-        piece = grads_v.at[1, :, pl.ds(CW * j, CW)]
-        grads_sib.append(send([(grads_hbm.at[:, pl.ds(CW * j, CW)], piece, sibling)], piece))
-    for copy in own[:3] + own[5:]:
-        copy.start()
-
-    own[3].wait()
-    mine = acts_v[:, pl.ds(pl.multiple_of(c * HALF, HALF), HALF)]
-    for k in range(2):
-        for t in range(2):
-            actst[256 * k:256 * k + 256, 256 * t:256 * t + 256] = (
-                mine[256 * t:256 * t + 256, 256 * k:256 * k + 256].T
-            )
+        sendc[j] = term(j).astype(BF)
+        rc.append(send([(sendc.at[j], recvc.at[j], sibling)], recvc.at[j]))
+    turn(c)
 
     own[0].wait()
     shifted[...] = jnp.zeros((8, 128), F32)
@@ -198,32 +203,17 @@
         mine = whole.at[pl.ds(2 * c, 2)]
         return gather(mine, [sibling], mine)
 
-    for copy in own[4:]:
+    for copy in own[5:]:
         copy.wait()
     basis_sib.wait_recv()
     a_first = first(abuf)
-
-    def term(slot, j):
-        part = dot(
-            actst[:, slot * TOK:slot * TOK + TOK], grads_v[slot, :, CW * j:CW * j + CW]
-        )
-        return part.reshape(NX, 128, CW)
-
-    for j in range(CHUNKS):
-        tbuf[j] = term(0, j)
-    acts_sib.wait_recv()
-    for k in range(2):
-        for t in range(2):
-            actst[256 * k:256 * k + 256, TOK + 256 * t:TOK + 256 * t + 256] = (
-                acts_sv[256 * t:256 * t + 256, 256 * k:256 * k + 256].T
-            )
 
     def pick():
         row = lax.broadcasted_iota(jnp.int32, (16, TOK), 0)
         col = lax.broadcasted_iota(jnp.int32, (16, TOK), 1)
         wanted = jnp.where(row == 0, idx_ref[0, 0], jnp.where(row == 1, idx_ref[0, 1], -1))
         hot = jnp.where(col == wanted, 1.0, 0.0).astype(BF)
-        for i, source in enumerate((acts_v[...], grads_v[0])):
+        for i, source in enumerate((acts_v[...], grads_v[...])):
             rows = dot(hot, source)
             for s in range(2):
                 for k in range(8):
@@ -243,8 +233,9 @@
         r2[j] = (up, down)
 
     for j in range(CHUNKS):
-        grads_sib[j].wait_recv()
-        tbuf[j] = tbuf[j] + term(1, j)
+        mine = term(j)
+        rc[j].wait_recv()
+        tbuf[j] = (mine + recvc[j].astype(F32)).reshape(NX, 128, CW)
         sendx1[j, 0, 0] = tbuf[j, x_far, 0:64, :].astype(BF)
         sendx1[j, 0, 1] = tbuf[j, x_up, 64:128, :].astype(BF)
         sendx1[j, 1, 0] = tbuf[j, x_far, 64:128, :].astype(BF)
@@ -426,9 +417,10 @@
             pltpu.VMEM((1, 32), F32),
             pltpu.VMEM((1, 128), F32),
             pltpu.VMEM((TOK, D), BF),
-            pltpu.VMEM((TOK, HALF), BF),
-            pltpu.VMEM((2, TOK, D), BF),
-            pltpu.VMEM((HALF, 2 * TOK), BF),
+            pltpu.VMEM((TOK, D), BF),
+            pltpu.VMEM((HALF, TOK), BF),
+            pltpu.VMEM((CHUNKS, HALF, CW), BF),
+            pltpu.VMEM((CHUNKS, HALF, CW), BF),
             pltpu.VMEM((4, NX, ZL, 64, 256), BF),
             pltpu.VMEM((CHUNKS, NX, 128, CW), F32),
             pltpu.VMEM((CHUNKS, 2, 2, 64, CW), BF),

time: 66.6 us -> 66.8 us (level)
  the two profiles are of different devices: /device:TPU:2 before, /device:TPU:1 now
where the time goes in v9:
time: 66.8 us; the launch traced here: 65.7 us
  Pallas kernels  65.1 us (97%)
    pallas_call x1, Pallas kernels, local(): pl.pallas_call(kernel, out_shape=jax.ShapeDtypeStruct((3, 32, D), BF), in...  63.3 us
    pallas_call x1, Pallas kernels, local(): pl.pallas_call(functools.partial(finish, act_scale=0.25 / total_samples,...  1.83 us

profile of v9, /device:TPU:1, one launch (start us, length us, event | category | flops | bytes accessed | tf_op | source)
XLA Modules:
  0.0 65.7 jit_solution(9093153427224082231)
XLA Ops:
  0.6 63.3 %shard_map.112.result_ref = bf16[3,32,1024]{2,1,0:T(8,128)(2,1)} custom-call(s32[1,2]{1,0:T(1,128)} %bitcast.4, bf16[512,1024]{1,0:T(8,128)(2,1)} %acts_hbm.1, bf16[512,1024]{1,0:T(8,128)(2,1)} %grads_hbm.1, bf16[32,1024]{1,0:T(8,128)(2,1)} %a_hbm.1, bf16[32,1024]{1,0:T(8,128)(2,1)} %b_hbm.1, f32[1,32]{1,0:T(1,128)} %bitcast.5, f32[1,1024]{1,0:T(1,128)} %bitcast.3), custom_call_target="tpu_custom_call" | custom-call | flops 2147483648 | bytes 2097152 | tf_op jit(solution)/shard_map/pallas_call | solution.py:409
  63.9 1.8 %shard_map.113 = (f32[32,1024]{1,0:T(8,128)}, f32[32,1024]{1,0:T(8,128)}, f32[32,1024]{1,0:T(8,128)}) custom-call(bf16[3,32,1024]{2,1,0:T(8,128)(2,1)} %shard_map.112.result_ref, f32[32,1024]{1,0:T(8,128)} %old_act_ref.1, f32[32,1024]{1,0:T(8,128)} %old_grad_ref.1), custom_call_target="tpu_custom_call" | custom-call | tf_op jit(solution)/shard_map/pallas_call | solution.py:469

commit v10 on v4

--- a/solution.py
+++ b/solution.py
@@ -84,10 +84,10 @@
     def gather(ref, targets, like):
         return send([(ref, ref, target) for target in targets], like)
 
-    def drain():
-        for copy in pending:
+    def drain(keep=0):
+        for copy in pending[:len(pending) - keep]:
             copy.wait_send()
-        pending.clear()
+        del pending[:len(pending) - keep]
 
     all_x = [to_x(s) for s in DX]
     all_y = [to_y(s) for s in DY]
@@ -124,6 +124,16 @@
         for h in range(2):
             moves.append((quarter(source, c, h), whole.at[2 * c + h, x, zl, my_rows]))
     own = [pltpu.make_async_copy(src, dst, lsem.at[i]) for i, (src, dst) in enumerate(moves)]
+    for copy in own[3:5]:
+        copy.start()
+    own[3].wait()
+    mine = acts_v[:, pl.ds(pl.multiple_of(c * HALF, HALF), HALF)]
+    for k in range(2):
+        for t in range(2):
+            actst[256 * k:256 * k + 256, 256 * t:256 * t + 256] = (
+                mine[256 * t:256 * t + 256, 256 * k:256 * k + 256].T
+            )
+
     pl.semaphore_wait(barrier, len(partners))
 
     basis_sib = []
@@ -141,7 +151,7 @@
     for j in range(CHUNKS):
         piece = grads_v.at[1, :, pl.ds(CW * j, CW)]
         grads_sib.append(send([(grads_hbm.at[:, pl.ds(CW * j, CW)], piece, sibling)], piece))
-    for copy in own:
+    for copy in own[:3] + own[5:]:
         copy.start()
 
     own[0].wait()
@@ -158,14 +168,6 @@
     for copy in own[1:3]:
         copy.wait()
     ez = gather(ebuf.at[x, zl, c], all_zl, ebuf.at[0, pl.ds(0, 3), 0])
-
-    own[3].wait()
-    mine = acts_v[:, pl.ds(pl.multiple_of(c * HALF, HALF), HALF)]
-    for k in range(2):
-        for t in range(2):
-            actst[256 * k:256 * k + 256, 256 * t:256 * t + 256] = (
-                mine[256 * t:256 * t + 256, 256 * k:256 * k + 256].T
-            )
 
     def first(whole):
         return (
@@ -366,6 +368,7 @@
     szsend[...] = stat
     sz = send([(szsend, szrecv, to_z(4))], szrecv)
 
+    drain(12)
     gxc.wait_recv()
     turned = gbuf[...].reshape(D, 128).T
     a_third.wait_recv()

time: 66.4 us -> 66.1 us (level)
  no operation moved by 1% of the time
where the time goes in v10:
time: 66.1 us; the launch traced here: 65.7 us
  Pallas kernels  65.1 us (98%)
    pallas_call x1, Pallas kernels, local(): pl.pallas_call(kernel, out_shape=jax.ShapeDtypeStruct((3, 32, D), F32), i...  63.2 us
    pallas_call x1, Pallas kernels, local(): pl.pallas_call(functools.partial(finish, act_scale=0.25 / total_samples,...  1.86 us

profile of v10, /device:TPU:1, one launch (start us, length us, event | category | flops | bytes accessed | tf_op | source)
XLA Modules:
  0.0 65.7 jit_solution(1549019782330324444)
XLA Ops:
  0.6 63.2 %shard_map.112.result_ref = f32[3,32,1024]{2,1,0:T(8,128)} custom-call(s32[1,2]{1,0:T(1,128)} %bitcast.4, bf16[512,1024]{1,0:T(8,128)(2,1)} %acts_hbm.1, bf16[512,1024]{1,0:T(8,128)(2,1)} %grads_hbm.1, bf16[32,1024]{1,0:T(8,128)(2,1)} %a_hbm.1, bf16[32,1024]{1,0:T(8,128)(2,1)} %b_hbm.1, f32[1,32]{1,0:T(1,128)} %bitcast.5, f32[1,1024]{1,0:T(1,128)} %bitcast.3), custom_call_target="tpu_custom_call" | custom-call | flops 2147483648 | bytes 2097152 | tf_op jit(solution)/shard_map/pallas_call | solution.py:422
  63.9 1.9 %shard_map.113 = (f32[32,1024]{1,0:T(8,128)}, f32[32,1024]{1,0:T(8,128)}, f32[32,1024]{1,0:T(8,128)}) custom-call(f32[3,32,1024]{2,1,0:T(8,128)} %shard_map.112.result_ref, f32[32,1024]{1,0:T(8,128)} %old_act_ref.1, f32[32,1024]{1,0:T(8,128)} %old_grad_ref.1), custom_call_target="tpu_custom_call" | custom-call | tf_op jit(solution)/shard_map/pallas_call | solution.py:480
